TPU v7x, 32 devices: a whole 2x2x4 slice. The times are simulated.
32 devices in a mesh: row: 4 (over y, x), blk: 8 (over z, core).
Axes of the slice: x: 2, y: 2, z: 4, core: 2. Of those that a mesh axis runs over, the one named last changes fastest.
Arguments:
- inputs: bfloat16 [4, 2048, 2048], P('row', 'blk'), may hold values from -6 to 6
- cotangent: bfloat16 [4, 2048, 2048], P('row', 'blk'), may hold values from -6 to 6
- doc_lengths: int32 [4, 8], P('row'), may hold values from 1 to 2041, as said below
- norm_gains: float32 [2, 2048], P(None, ('row', 'blk')), may hold values from 0.5 to 1.5
- gain_first: float32 [2, 2048], P(None, ('row', 'blk')), may hold values from -56 to 56
- gain_second: float32 [2, 2048], P(None, ('row', 'blk')), may hold values from 1228.8 to 4915.2
- query_weight: float32 [32, 512, 256], P(('row', 'blk')), may hold values from -0.125 to 0.125
- query_left: float32 [32, 512, 512], P(('row', 'blk')), as said below
- query_right: float32 [32, 256, 256], P(('row', 'blk')), as said below
- query_leftroot: float32 [32, 512, 512], P(('row', 'blk')), as said below
- query_rightroot: float32 [32, 256, 256], P(('row', 'blk')), as said below
- key_weight: float32 [32, 256, 128], P(('row', 'blk')), may hold values from -0.125 to 0.125
- key_left: float32 [32, 256, 256], P(('row', 'blk')), as said below
- key_right: float32 [32, 128, 128], P(('row', 'blk')), as said below
- key_leftroot: float32 [32, 256, 256], P(('row', 'blk')), as said below
- key_rightroot: float32 [32, 128, 128], P(('row', 'blk')), as said below
- value_weight: float32 [32, 256, 128], P(('row', 'blk')), may hold values from -0.125 to 0.125
- value_left: float32 [32, 256, 256], P(('row', 'blk')), as said below
- value_right: float32 [32, 128, 128], P(('row', 'blk')), as said below
- value_leftroot: float32 [32, 256, 256], P(('row', 'blk')), as said below
- value_rightroot: float32 [32, 128, 128], P(('row', 'blk')), as said below
- output_weight: float32 [32, 256, 512], P(('row', 'blk')), may hold values from -4 to 4
- output_left: float32 [32, 256, 256], P(('row', 'blk')), as said below
- output_right: float32 [32, 512, 512], P(('row', 'blk')), as said below
- output_leftroot: float32 [32, 256, 256], P(('row', 'blk')), as said below
- output_rightroot: float32 [32, 512, 512], P(('row', 'blk')), as said below
- gate_weight: float32 [32, 512, 1024], P(('row', 'blk')), may hold values from -0.125 to 0.125
- gate_left: float32 [32, 512, 512], P(('row', 'blk')), as said below
- gate_right: float32 [32, 1024, 1024], P(('row', 'blk')), as said below
- gate_leftroot: float32 [32, 512, 512], P(('row', 'blk')), as said below
- gate_rightroot: float32 [32, 1024, 1024], P(('row', 'blk')), as said below
- up_weight: float32 [32, 512, 1024], P(('row', 'blk')), may hold values from -0.125 to 0.125
- up_left: float32 [32, 512, 512], P(('row', 'blk')), as said below
- up_right: float32 [32, 1024, 1024], P(('row', 'blk')), as said below
- up_leftroot: float32 [32, 512, 512], P(('row', 'blk')), as said below
- up_rightroot: float32 [32, 1024, 1024], P(('row', 'blk')), as said below
- down_weight: float32 [32, 1024, 512], P(('row', 'blk')), may hold values from -0.0625 to 0.0625
- down_left: float32 [32, 1024, 1024], P(('row', 'blk')), as said below
- down_right: float32 [32, 512, 512], P(('row', 'blk')), as said below
- down_leftroot: float32 [32, 1024, 1024], P(('row', 'blk')), as said below
- down_rightroot: float32 [32, 512, 512], P(('row', 'blk')), as said below
Outputs:
- block_out: bfloat16 [4, 2048, 2048], P('row', 'blk')
- input_grad: float32 [4, 2048, 2048], P('row', 'blk')
- query_grad: float32 [32, 512, 256], P(('row', 'blk'))
- query_new: float32 [32, 512, 256], P(('row', 'blk'))
- query_leftnew: float32 [32, 512, 512], P(('row', 'blk'))
- query_rightnew: float32 [32, 256, 256], P(('row', 'blk'))
- key_grad: float32 [32, 256, 128], P(('row', 'blk'))
- key_new: float32 [32, 256, 128], P(('row', 'blk'))
- key_leftnew: float32 [32, 256, 256], P(('row', 'blk'))
- key_rightnew: float32 [32, 128, 128], P(('row', 'blk'))
- value_grad: float32 [32, 256, 128], P(('row', 'blk'))
- value_new: float32 [32, 256, 128], P(('row', 'blk'))
- value_leftnew: float32 [32, 256, 256], P(('row', 'blk'))
- value_rightnew: float32 [32, 128, 128], P(('row', 'blk'))
- output_grad: float32 [32, 256, 512], P(('row', 'blk'))
- output_new: float32 [32, 256, 512], P(('row', 'blk'))
- output_leftnew: float32 [32, 256, 256], P(('row', 'blk'))
- output_rightnew: float32 [32, 512, 512], P(('row', 'blk'))
- gate_grad: float32 [32, 512, 1024], P(('row', 'blk'))
- gate_new: float32 [32, 512, 1024], P(('row', 'blk'))
- gate_leftnew: float32 [32, 512, 512], P(('row', 'blk'))
- gate_rightnew: float32 [32, 1024, 1024], P(('row', 'blk'))
- up_grad: float32 [32, 512, 1024], P(('row', 'blk'))
- up_new: float32 [32, 512, 1024], P(('row', 'blk'))
- up_leftnew: float32 [32, 512, 512], P(('row', 'blk'))
- up_rightnew: float32 [32, 1024, 1024], P(('row', 'blk'))
- down_grad: float32 [32, 1024, 512], P(('row', 'blk'))
- down_new: float32 [32, 1024, 512], P(('row', 'blk'))
- down_leftnew: float32 [32, 1024, 1024], P(('row', 'blk'))
- down_rightnew: float32 [32, 512, 512], P(('row', 'blk'))
- gain_moment: float32 [2, 2048], P(None, ('row', 'blk'))
- gain_square: float32 [2, 2048], P(None, ('row', 'blk'))
- gains_new: float32 [2, 2048], P(None, ('row', 'blk'))
Inputs may be any that keep to these rules, and one draw needn't show every extreme that they name: `doc_lengths`: the 8 lengths of each row sum to 2048. `query_left`: symmetric, one matrix for each block. `query_right`: symmetric, one matrix for each block. `query_leftroot`: symmetric, one matrix for each block. `query_rightroot`: symmetric, one matrix for each block. `key_left`: symmetric, one matrix for each block. `key_right`: symmetric, one matrix for each block. `key_leftroot`: symmetric, one matrix for each block. `key_rightroot`: symmetric, one matrix for each block. `value_left`: symmetric, one matrix for each block. `value_right`: symmetric, one matrix for each block. `value_leftroot`: symmetric, one matrix for each block. `value_rightroot`: symmetric, one matrix for each block. `output_left`: symmetric, one matrix for each block. `output_right`: symmetric, one matrix for each block. `output_leftroot`: symmetric, one matrix for each block. `output_rightroot`: symmetric, one matrix for each block. `gate_left`: symmetric, one matrix for each block. `gate_right`: symmetric, one matrix for each block. `gate_leftroot`: symmetric, one matrix for each block. `gate_rightroot`: symmetric, one matrix for each block. `up_left`: symmetric, one matrix for each block. `up_right`: symmetric, one matrix for each block. `up_leftroot`: symmetric, one matrix for each block. `up_rightroot`: symmetric, one matrix for each block. `down_left`: symmetric, one matrix for each block. `down_right`: symmetric, one matrix for each block. `down_leftroot`: symmetric, one matrix for each block. `down_rightroot`: symmetric, one matrix for each block.
All inputs are finite; a program needn't handle non-finite values.
Results may differ from a plain program's by a relative error of at most 0.023.
Values may be sent and summed in bfloat16 or wider, within the bound.
No kernel may reach another device: no remote copies, remote signals or barrier semaphores. Data moves between devices by JAX's collectives and lax.ppermute only.
A program may use at most 640 MiB of HBM per device.

v0:
```python
import math

import jax
import jax.numpy as jnp
from jax import lax
from jax.sharding import PartitionSpec as P

HEADS = 32
KV_HEADS = 8
HEAD_DIM = 64
STEP = 10


NORM_EPSILON = 1e-05
ROPE_THETA = 500000.0
ROPE_FACTOR = 32.0
LOW_FACTOR = 1.0
HIGH_FACTOR = 4.0
BASE_SPAN = 8192.0
SCORE_SCALE = 0.125
MASKED = -1e30
SHAMPOO_DECAY = 0.95
SHAMPOO_RATE = 0.5
ADAM_RATE = 1.0
ADAM_FIRST = 0.9
ADAM_SECOND = 0.95
ADAM_EPSILON = 1e-08
HIGHEST = lax.Precision.HIGHEST


def rope_rates():
    exponents = jnp.arange(0, HEAD_DIM, 2).astype(jnp.float32) / HEAD_DIM
    base_rates = 1.0 / ROPE_THETA**exponents
    wavelength = 2.0 * math.pi / base_rates
    smooth = (BASE_SPAN / wavelength - LOW_FACTOR) / (HIGH_FACTOR - LOW_FACTOR)
    blended = (1.0 - smooth) * base_rates / ROPE_FACTOR + smooth * base_rates
    longer = jnp.where(wavelength > BASE_SPAN / LOW_FACTOR, base_rates / ROPE_FACTOR, blended)
    return jnp.where(wavelength < BASE_SPAN / HIGH_FACTOR, base_rates, longer)


def rotate(vectors, cos_table, sin_table):
    half_dim = vectors.shape[-1] // 2
    former = vectors[..., :half_dim]
    latter = vectors[..., half_dim:]
    return jnp.concatenate(
        [former * cos_table - latter * sin_table, latter * cos_table + former * sin_table], axis=-1
    )


def unrotate(gradient, cos_table, sin_table):
    half_dim = gradient.shape[-1] // 2
    former = gradient[..., :half_dim]
    latter = gradient[..., half_dim:]
    return jnp.concatenate(
        [former * cos_table + latter * sin_table, latter * cos_table - former * sin_table], axis=-1
    )


def project(activations, blocks, rows_first):
    row_parts, col_parts, size_in, size_out = blocks.shape
    if rows_first:
        shaped = activations.reshape(-1, row_parts, size_in)
        return jnp.einsum(
            "tri,rcij->tcj", shaped, blocks, preferred_element_type=jnp.float32
        ).reshape(-1, col_parts * size_out)
    shaped = activations.reshape(-1, col_parts, size_in)
    return jnp.einsum("tci,rcij->trj", shaped, blocks, preferred_element_type=jnp.float32).reshape(
        -1, row_parts * size_out
    )


def project_back(gradient, blocks, rows_first):
    row_parts, col_parts, size_in, size_out = blocks.shape
    if rows_first:
        shaped = gradient.reshape(-1, col_parts, size_out)
        return jnp.einsum(
            "tcj,rcij->tri", shaped, blocks, preferred_element_type=jnp.float32
        ).reshape(-1, row_parts * size_in)
    shaped = gradient.reshape(-1, row_parts, size_out)
    return jnp.einsum("trj,rcij->tci", shaped, blocks, preferred_element_type=jnp.float32).reshape(
        -1, col_parts * size_in
    )


def block_grad(activations, gradient, row_parts, col_parts, rows_first):
    token_count = activations.shape[0]
    if rows_first:
        result = jnp.einsum(
            "tri,tcj->rcij",
            activations.reshape(token_count, row_parts, -1),
            gradient.reshape(token_count, col_parts, -1),
            preferred_element_type=jnp.float32,
        )
    else:
        result = jnp.einsum(
            "tci,trj->rcij",
            activations.reshape(token_count, col_parts, -1),
            gradient.reshape(token_count, row_parts, -1),
            preferred_element_type=jnp.float32,
        )
    return result.reshape(row_parts * col_parts, result.shape[2], result.shape[3])


def shampoo_step(gradient, master, left, right, left_root, right_root):
    left_new = SHAMPOO_DECAY * left + (1.0 - SHAMPOO_DECAY) * jnp.einsum(
        "nab,ncb->nac", gradient, gradient, precision=HIGHEST
    )
    right_new = SHAMPOO_DECAY * right + (1.0 - SHAMPOO_DECAY) * jnp.einsum(
        "nab,nac->nbc", gradient, gradient, precision=HIGHEST
    )
    turned = jnp.einsum("nab,nbc->nac", left_root, gradient, precision=HIGHEST)
    direction = jnp.einsum("nab,nbc->nac", turned, right_root, precision=HIGHEST)
    return (gradient, master - SHAMPOO_RATE * direction, left_new, right_new)


def adam_step(gradient, gains, first, second):
    first_new = ADAM_FIRST * first + (1.0 - ADAM_FIRST) * gradient
    second_new = ADAM_SECOND * second + (1.0 - ADAM_SECOND) * gradient * gradient
    corrected_first = first_new / (1.0 - ADAM_FIRST**STEP)
    corrected_second = second_new / (1.0 - ADAM_SECOND**STEP)
    return (
        first_new,
        second_new,
        gains - ADAM_RATE * corrected_first / (jnp.sqrt(corrected_second) + ADAM_EPSILON),
    )


def masked_scores(queries, key_block, block_start, query_index, query_begin):
    row_count = key_block.shape[0]
    scores = (
        jnp.einsum("tkgd,skd->kgts", queries, key_block, preferred_element_type=jnp.float32)
        * SCORE_SCALE
    )
    key_index = block_start + jnp.arange(row_count, dtype=jnp.int32)
    allowed = (key_index[None, :] >= query_begin[:, None]) & (
        key_index[None, :] <= query_index[:, None]
    )
    return (scores, allowed)


def forward_block(carried, key_block, value_block, block_start, queries, query_index, query_begin):
    maxima, totals, accumulated = carried
    scores, allowed = masked_scores(queries, key_block, block_start, query_index, query_begin)
    scores = jnp.where(allowed, scores, MASKED)
    peaks = jnp.maximum(maxima, jnp.max(scores, axis=-1))
    weights_now = jnp.where(allowed, jnp.exp(scores - peaks[..., None]), 0.0)
    factor = jnp.exp(maxima - peaks)
    totals = totals * factor + jnp.sum(weights_now, axis=-1)
    accumulated = accumulated * jnp.moveaxis(factor, 2, 0)[..., None] + jnp.einsum(
        "kgts,skd->tkgd",
        weights_now.astype(jnp.bfloat16),
        value_block,
        preferred_element_type=jnp.float32,
    )
    return (peaks, totals, accumulated)


def backward_block(
    carried,
    key_block,
    value_block,
    block_start,
    queries,
    query_index,
    query_begin,
    log_totals,
    deltas,
    out_grad,
):
    query_rot, key_all, value_all = carried
    row_count = key_block.shape[0]
    scores, allowed = masked_scores(queries, key_block, block_start, query_index, query_begin)
    probabilities = jnp.where(allowed, jnp.exp(scores - log_totals[..., None]), 0.0)
    prob_grads = jnp.einsum(
        "tkgd,skd->kgts", out_grad, value_block, preferred_element_type=jnp.float32
    )
    score_grads = (probabilities * (prob_grads - deltas[..., None])).astype(jnp.bfloat16)
    query_rot = query_rot + SCORE_SCALE * jnp.einsum(
        "kgts,skd->tkgd", score_grads, key_block, preferred_element_type=jnp.float32
    )
    key_part = SCORE_SCALE * jnp.einsum(
        "kgts,tkgd->skd", score_grads, queries, preferred_element_type=jnp.float32
    )
    value_part = jnp.einsum(
        "kgts,tkgd->skd",
        probabilities.astype(jnp.bfloat16),
        out_grad,
        preferred_element_type=jnp.float32,
    )
    key_all = lax.dynamic_update_slice_in_dim(
        key_all,
        lax.dynamic_slice_in_dim(key_all, block_start, row_count, 0) + key_part,
        block_start,
        0,
    )
    value_all = lax.dynamic_update_slice_in_dim(
        value_all,
        lax.dynamic_slice_in_dim(value_all, block_start, row_count, 0) + value_part,
        block_start,
        0,
    )
    return (query_rot, key_all, value_all)


def sweep_keys(carried, key_rows, value_rows, visit, query_last, first_begin):
    row_count = key_rows.shape[0]
    block_rows = math.gcd(row_count, 512)

    def visit_block(number, state):
        offset = number * block_rows
        key_block = lax.dynamic_slice_in_dim(key_rows, offset, block_rows, 0)
        value_block = lax.dynamic_slice_in_dim(value_rows, offset, block_rows, 0)
        needed = (offset <= query_last) & (offset + block_rows - 1 >= first_begin)
        return lax.cond(
            needed,
            lambda inner: visit(inner, key_block, value_block, offset),
            lambda inner: inner,
            state,
        )

    return lax.fori_loop(0, row_count // block_rows, visit_block, carried)


def shards(
    inputs,
    cotangent,
    doc_lengths,
    norm_gains,
    gain_first,
    gain_second,
    query_weight,
    query_left,
    query_right,
    query_leftroot,
    query_rightroot,
    key_weight,
    key_left,
    key_right,
    key_leftroot,
    key_rightroot,
    value_weight,
    value_left,
    value_right,
    value_leftroot,
    value_rightroot,
    output_weight,
    output_left,
    output_right,
    output_leftroot,
    output_rightroot,
    gate_weight,
    gate_left,
    gate_right,
    gate_leftroot,
    gate_rightroot,
    up_weight,
    up_left,
    up_right,
    up_leftroot,
    up_rightroot,
    down_weight,
    down_left,
    down_right,
    down_leftroot,
    down_rightroot,
):
    row_parts = lax.axis_size("row")
    block_parts = lax.axis_size("blk")
    gathered = (
        lax.all_gather(query_weight.astype(jnp.bfloat16), ("row", "blk"), axis=0, tiled=True),
        lax.all_gather(key_weight.astype(jnp.bfloat16), ("row", "blk"), axis=0, tiled=True),
        lax.all_gather(value_weight.astype(jnp.bfloat16), ("row", "blk"), axis=0, tiled=True),
        lax.all_gather(output_weight.astype(jnp.bfloat16), ("row", "blk"), axis=0, tiled=True),
        lax.all_gather(gate_weight.astype(jnp.bfloat16), ("row", "blk"), axis=0, tiled=True),
        lax.all_gather(up_weight.astype(jnp.bfloat16), ("row", "blk"), axis=0, tiled=True),
        lax.all_gather(down_weight.astype(jnp.bfloat16), ("row", "blk"), axis=0, tiled=True),
        lax.all_gather(norm_gains.astype(jnp.bfloat16), ("row", "blk"), axis=1, tiled=True),
    )

    def arrange(shard):
        return shard.reshape(row_parts, block_parts, shard.shape[1], shard.shape[2])

    query_full = arrange(gathered[0])
    key_full = arrange(gathered[1])
    value_full = arrange(gathered[2])
    output_full = arrange(gathered[3])
    gate_full = arrange(gathered[4])
    up_full = arrange(gathered[5])
    down_full = arrange(gathered[6])
    gains_full = gathered[7].astype(jnp.float32)
    token_count = inputs.shape[1]
    seq_total = token_count * block_parts
    group_size = HEADS // KV_HEADS
    resid = inputs[0].astype(jnp.float32)
    query_index = lax.axis_index("blk") * token_count + jnp.arange(token_count, dtype=jnp.int32)
    lengths_row = doc_lengths[0]
    doc_ends = jnp.cumsum(lengths_row)
    doc_starts = doc_ends - lengths_row
    inside = (query_index[:, None] >= doc_starts[None, :]) & (
        query_index[:, None] < doc_ends[None, :]
    )
    query_begin = jnp.sum(jnp.where(inside, doc_starts[None, :], 0), axis=-1)
    angles = (query_index - query_begin).astype(jnp.float32)[:, None] * rope_rates()[None, :]
    cos_table = jnp.cos(angles)[:, None, :]
    sin_table = jnp.sin(angles)[:, None, :]
    query_last = query_index[token_count - 1]
    first_begin = query_begin[0]
    inverse_first = lax.rsqrt(jnp.mean(resid * resid, axis=-1, keepdims=True) + NORM_EPSILON)
    normed_first = resid * inverse_first
    scaled_first = (normed_first * gains_full[0]).astype(jnp.bfloat16)
    query_pre = project(scaled_first, query_full, True)
    key_pre = project(scaled_first, key_full, False)
    value_rows = (
        project(scaled_first, value_full, False)
        .astype(jnp.bfloat16)
        .reshape(token_count, KV_HEADS, HEAD_DIM)
    )
    queries = rotate(query_pre.reshape(token_count, HEADS, HEAD_DIM), cos_table, sin_table).astype(
        jnp.bfloat16
    )
    queries = queries.reshape(token_count, KV_HEADS, group_size, HEAD_DIM)
    key_rows = rotate(
        key_pre.reshape(token_count, KV_HEADS, HEAD_DIM), cos_table, sin_table
    ).astype(jnp.bfloat16)
    start_state = (
        jnp.full((KV_HEADS, group_size, token_count), MASKED, jnp.float32),
        jnp.zeros((KV_HEADS, group_size, token_count), jnp.float32),
        jnp.zeros((token_count, KV_HEADS, group_size, HEAD_DIM), jnp.float32),
    )

    def forward_visit(carried, key_block, value_block, block_start):
        return forward_block(
            carried, key_block, value_block, block_start, queries, query_index, query_begin
        )

    piece = (
        lax.all_gather(key_rows, "blk", axis=0, tiled=True),
        lax.all_gather(value_rows, "blk", axis=0, tiled=True),
    )
    maxima, totals, accumulated = sweep_keys(
        start_state, piece[0], piece[1], forward_visit, query_last, first_begin
    )
    attended = accumulated / jnp.moveaxis(totals, 2, 0)[..., None]
    log_totals = maxima + jnp.log(totals)
    attended_low = attended.reshape(token_count, HEADS * HEAD_DIM).astype(jnp.bfloat16)
    residual = resid + project(attended_low, output_full, False)
    inverse_second = lax.rsqrt(jnp.mean(residual * residual, axis=-1, keepdims=True) + NORM_EPSILON)
    normed_second = residual * inverse_second
    scaled_second = (normed_second * gains_full[1]).astype(jnp.bfloat16)
    gate_pre = project(scaled_second, gate_full, True)
    up_pre = project(scaled_second, up_full, True)
    sigmoid_gate = jax.nn.sigmoid(gate_pre)
    silu_gate = gate_pre * sigmoid_gate
    hidden = (silu_gate * up_pre).astype(jnp.bfloat16)
    result = residual + project(hidden, down_full, False)
    block_out = result.astype(jnp.bfloat16)[None]
    upstream = cotangent[0]
    down_grad = block_grad(hidden, upstream, row_parts, block_parts, False)
    hidden_grad = project_back(upstream, down_full, False)
    gate_low = (
        hidden_grad * up_pre * sigmoid_gate * (1.0 + gate_pre * (1.0 - sigmoid_gate))
    ).astype(jnp.bfloat16)
    up_low = (hidden_grad * silu_gate).astype(jnp.bfloat16)
    gate_grad = block_grad(scaled_second, gate_low, row_parts, block_parts, True)
    up_grad = block_grad(scaled_second, up_low, row_parts, block_parts, True)
    scaled_second_grad = project_back(gate_low, gate_full, True) + project_back(
        up_low, up_full, True
    )
    gain_second_grad = jnp.sum(scaled_second_grad * normed_second, axis=0)
    normed_second_grad = scaled_second_grad * gains_full[1]
    residual_grad = upstream.astype(jnp.float32) + inverse_second * (
        normed_second_grad
        - normed_second * jnp.mean(normed_second_grad * normed_second, axis=-1, keepdims=True)
    )
    residual_low = residual_grad.astype(jnp.bfloat16)
    output_grad = block_grad(attended_low, residual_low, row_parts, block_parts, False)
    out_grad = project_back(residual_low, output_full, False).astype(jnp.bfloat16)
    out_grad = out_grad.reshape(token_count, KV_HEADS, group_size, HEAD_DIM)
    deltas = jnp.moveaxis(jnp.sum(out_grad.astype(jnp.float32) * attended, axis=-1), 0, 2)
    back_state = (
        jnp.zeros((token_count, KV_HEADS, group_size, HEAD_DIM), jnp.float32),
        jnp.zeros((seq_total, KV_HEADS, HEAD_DIM), jnp.float32),
        jnp.zeros((seq_total, KV_HEADS, HEAD_DIM), jnp.float32),
    )

    def backward_visit(carried, key_block, value_block, block_start):
        return backward_block(
            carried,
            key_block,
            value_block,
            block_start,
            queries,
            query_index,
            query_begin,
            log_totals,
            deltas,
            out_grad,
        )

    piece = (
        lax.all_gather(key_rows, "blk", axis=0, tiled=True),
        lax.all_gather(value_rows, "blk", axis=0, tiled=True),
    )
    query_rot, key_all, value_all = sweep_keys(
        back_state, piece[0], piece[1], backward_visit, query_last, first_begin
    )
    key_rot, value_local = (
        lax.psum_scatter(
            key_all.astype(jnp.bfloat16), "blk", scatter_dimension=0, tiled=True
        ).astype(jnp.float32),
        lax.psum_scatter(
            value_all.astype(jnp.bfloat16), "blk", scatter_dimension=0, tiled=True
        ).astype(jnp.float32),
    )
    query_low = unrotate(query_rot.reshape(token_count, HEADS, HEAD_DIM), cos_table, sin_table)
    query_low = query_low.reshape(token_count, HEADS * HEAD_DIM).astype(jnp.bfloat16)
    key_low = (
        unrotate(key_rot, cos_table, sin_table)
        .reshape(token_count, KV_HEADS * HEAD_DIM)
        .astype(jnp.bfloat16)
    )
    value_low = value_local.reshape(token_count, KV_HEADS * HEAD_DIM).astype(jnp.bfloat16)
    query_grad = block_grad(scaled_first, query_low, row_parts, block_parts, True)
    key_grad = block_grad(scaled_first, key_low, row_parts, block_parts, False)
    value_grad = block_grad(scaled_first, value_low, row_parts, block_parts, False)
    scaled_first_grad = (
        project_back(query_low, query_full, True)
        + project_back(key_low, key_full, False)
        + project_back(value_low, value_full, False)
    )
    gain_first_grad = jnp.sum(scaled_first_grad * normed_first, axis=0)
    normed_first_grad = scaled_first_grad * gains_full[0]
    input_grad = residual_grad + inverse_first * (
        normed_first_grad
        - normed_first * jnp.mean(normed_first_grad * normed_first, axis=-1, keepdims=True)
    )
    every_sum = (
        lax.psum_scatter(query_grad, ("row", "blk"), scatter_dimension=0, tiled=True),
        lax.psum_scatter(key_grad, ("row", "blk"), scatter_dimension=0, tiled=True),
        lax.psum_scatter(value_grad, ("row", "blk"), scatter_dimension=0, tiled=True),
        lax.psum_scatter(output_grad, ("row", "blk"), scatter_dimension=0, tiled=True),
        lax.psum_scatter(gate_grad, ("row", "blk"), scatter_dimension=0, tiled=True),
        lax.psum_scatter(up_grad, ("row", "blk"), scatter_dimension=0, tiled=True),
        lax.psum_scatter(down_grad, ("row", "blk"), scatter_dimension=0, tiled=True),
        lax.psum_scatter(
            jnp.stack([gain_first_grad, gain_second_grad]),
            ("row", "blk"),
            scatter_dimension=1,
            tiled=True,
        ),
    )
    summed = (
        every_sum[0],
        every_sum[1],
        every_sum[2],
        every_sum[3],
        every_sum[4],
        every_sum[5],
        every_sum[6],
    )
    gains_summed = every_sum[7]
    query_out = shampoo_step(
        summed[0], query_weight, query_left, query_right, query_leftroot, query_rightroot
    )
    key_out = shampoo_step(summed[1], key_weight, key_left, key_right, key_leftroot, key_rightroot)
    value_out = shampoo_step(
        summed[2], value_weight, value_left, value_right, value_leftroot, value_rightroot
    )
    output_out = shampoo_step(
        summed[3], output_weight, output_left, output_right, output_leftroot, output_rightroot
    )
    gate_out = shampoo_step(
        summed[4], gate_weight, gate_left, gate_right, gate_leftroot, gate_rightroot
    )
    up_out = shampoo_step(summed[5], up_weight, up_left, up_right, up_leftroot, up_rightroot)
    down_out = shampoo_step(
        summed[6], down_weight, down_left, down_right, down_leftroot, down_rightroot
    )
    gain_out = adam_step(gains_summed, norm_gains, gain_first, gain_second)
    return (
        block_out,
        input_grad[None],
        query_out[0],
        query_out[1],
        query_out[2],
        query_out[3],
        key_out[0],
        key_out[1],
        key_out[2],
        key_out[3],
        value_out[0],
        value_out[1],
        value_out[2],
        value_out[3],
        output_out[0],
        output_out[1],
        output_out[2],
        output_out[3],
        gate_out[0],
        gate_out[1],
        gate_out[2],
        gate_out[3],
        up_out[0],
        up_out[1],
        up_out[2],
        up_out[3],
        down_out[0],
        down_out[1],
        down_out[2],
        down_out[3],
        gain_out[0],
        gain_out[1],
        gain_out[2],
    )


def solution(mesh):
    placed = (
        P("row", "blk", None),
        P("row", "blk", None),
        P("row", None),
        P(None, ("row", "blk")),
        P(None, ("row", "blk")),
        P(None, ("row", "blk")),
        P(("row", "blk"), None, None),
        P(("row", "blk"), None, None),
        P(("row", "blk"), None, None),
        P(("row", "blk"), None, None),
        P(("row", "blk"), None, None),
        P(("row", "blk"), None, None),
        P(("row", "blk"), None, None),
        P(("row", "blk"), None, None),
        P(("row", "blk"), None, None),
        P(("row", "blk"), None, None),
        P(("row", "blk"), None, None),
        P(("row", "blk"), None, None),
        P(("row", "blk"), None, None),
        P(("row", "blk"), None, None),
        P(("row", "blk"), None, None),
        P(("row", "blk"), None, None),
        P(("row", "blk"), None, None),
        P(("row", "blk"), None, None),
        P(("row", "blk"), None, None),
        P(("row", "blk"), None, None),
        P(("row", "blk"), None, None),
        P(("row", "blk"), None, None),
        P(("row", "blk"), None, None),
        P(("row", "blk"), None, None),
        P(("row", "blk"), None, None),
        P(("row", "blk"), None, None),
        P(("row", "blk"), None, None),
        P(("row", "blk"), None, None),
        P(("row", "blk"), None, None),
        P(("row", "blk"), None, None),
        P(("row", "blk"), None, None),
        P(("row", "blk"), None, None),
        P(("row", "blk"), None, None),
        P(("row", "blk"), None, None),
        P(("row", "blk"), None, None),
    )
    return jax.shard_map(
        shards,
        mesh=mesh,
        in_specs=placed,
        out_specs=(
            P("row", "blk", None),
            P("row", "blk", None),
            P(("row", "blk"), None, None),
            P(("row", "blk"), None, None),
            P(("row", "blk"), None, None),
            P(("row", "blk"), None, None),
            P(("row", "blk"), None, None),
            P(("row", "blk"), None, None),
            P(("row", "blk"), None, None),
            P(("row", "blk"), None, None),
            P(("row", "blk"), None, None),
            P(("row", "blk"), None, None),
            P(("row", "blk"), None, None),
            P(("row", "blk"), None, None),
            P(("row", "blk"), None, None),
            P(("row", "blk"), None, None),
            P(("row", "blk"), None, None),
            P(("row", "blk"), None, None),
            P(("row", "blk"), None, None),
            P(("row", "blk"), None, None),
            P(("row", "blk"), None, None),
            P(("row", "blk"), None, None),
            P(("row", "blk"), None, None),
            P(("row", "blk"), None, None),
            P(("row", "blk"), None, None),
            P(("row", "blk"), None, None),
            P(("row", "blk"), None, None),
            P(("row", "blk"), None, None),
            P(("row", "blk"), None, None),
            P(("row", "blk"), None, None),
            P(None, ("row", "blk")),
            P(None, ("row", "blk")),
            P(None, ("row", "blk")),
        ),
        check_vma=False,
    )
```

profile of v0, /device:TPU:0, one launch (start us, length us, event | category | flops | bytes accessed | tf_op | source)
XLA Modules:
  0.0 4245.5 jit_solution(11961126568371989950)
XLA Ops:
  15.1 43.0 %all-gather = bf16[32,64,2]{1,2,0:T(2,128)(2,1)S(1)} all-gather(bf16[1,64,2]{1,2,0:T(2,128)(2,1)S(1)} %convert_bitcast_fusion), channel_id=1, replica_groups=mesh['row'=4,'blk'=8] {'row','blk'}, dimensions={0}, use_global_device_ids=true | all-gather | bytes 8448 | tf_op jit(solution)/shard_map/all_gather | solution.py:277
  78.8 51.1 %all-gather.17.cloned.1.call-done = bf16[32,256,128]{2,1,0:T(8,128)(2,1)} async-done(((bf16[1,256,128]{2,1,0:T(8,128)(2,1)}), bf16[32,256,128]{2,1,0:T(8,128)(2,1)}) %all-gather.17.cloned.1.call-update) | async-done | bytes 2097168 | tf_op jit(solution)/shard_map/all_gather | solution.py:272
  151.2 58.5 %all-gather.21.cloned.1.call-done = bf16[32,256,512]{2,1,0:T(8,128)(2,1)} async-done(((bf16[1,256,512]{2,1,0:T(8,128)(2,1)}), bf16[32,256,512]{2,1,0:T(8,128)(2,1)}) %all-gather.21.cloned.1.call-update) | async-done | bytes 8388624 | tf_op jit(solution)/shard_map/all_gather | solution.py:273
  221.8 67.3 %all-gather.15.cloned.1.call-done = bf16[32,512,256]{2,1,0:T(8,128)(2,1)} async-done(((bf16[1,512,256]{2,1,0:T(8,128)(2,1)}), bf16[32,512,256]{2,1,0:T(8,128)(2,1)}) %all-gather.15.cloned.1.call-update) | async-done | bytes 8388624 | tf_op jit(solution)/shard_map/all_gather | solution.py:270
  320.5 32.0 all-gather.19.cloned.1.call-done
  383.8 166.2 %all-gather.23.cloned.1.call-done = bf16[32,512,1024]{2,1,0:T(8,128)(2,1)} async-done(((bf16[1,512,1024]{2,1,0:T(8,128)(2,1)}), bf16[32,512,1024]{2,1,0:T(8,128)(2,1)}) %all-gather.23.cloned.1.call-update) | async-done | bytes 33554448 | tf_op jit(solution)/shard_map/all_gather | solution.py:274
  549.9 42.2 copy.337
  616.0 130.5 %all-gather.25.cloned.1.call-done = bf16[32,512,1024]{2,1,0:T(8,128)(2,1)} async-done(((bf16[1,512,1024]{2,1,0:T(8,128)(2,1)}), bf16[32,512,1024]{2,1,0:T(8,128)(2,1)}) %all-gather.25.cloned.1.call-update) | async-done | bytes 33554448 | tf_op jit(solution)/shard_map/all_gather | solution.py:275
  746.5 42.2 copy.339
  850.1 93.0 %all-gather.27.cloned.1.call-done = bf16[32,1024,512]{2,1,0:T(8,128)(2,1)} async-done(((bf16[1,1024,512]{2,1,0:T(8,128)(2,1)}), bf16[32,1024,512]{2,1,0:T(8,128)(2,1)}) %all-gather.27.cloned.1.call-update) | async-done | bytes 33554448 | tf_op jit(solution)/shard_map/all_gather | solution.py:276
  1019.6 41.8 while.45
  1021.1 36.3 conditional.7
  1078.6 129.3 %reduce-scatter.13.cloned.1.call-done = bf16[256,8,64]{0,2,1:T(8,128)(2,1)} async-done(((bf16[2048,8,64]{0,2,1:T(8,128)(2,1)}), bf16[256,8,64]{0,2,1:T(8,128)(2,1)}) %reduce-scatter.13.cloned.1.call-update) | async-done | bytes 262160 | tf_op jit(solution)/shard_map/reduce_scatter | solution.py:408
  1212.8 32.4 reduce-scatter.15.cloned.1.call-done
  1363.7 63.4 %copy.368 = f32[4,8,512,1024]{3,2,1,0:T(8,128)} copy(f32[4,8,512,1024]{2,3,0,1:T(8,128)} %convolution_bitcast_fusion.2) | data formatting | bytes 134217728 | tf_op jit(solution)/shard_map/tri,tcj->rcij/transpose | solution.py:88
  1459.1 63.4 %copy.365 = f32[4,8,512,1024]{3,2,1,0:T(8,128)} copy(f32[4,8,512,1024]{2,3,0,1:T(8,128)} %convolution_bitcast_fusion.3) | data formatting | bytes 134217728 | tf_op jit(solution)/shard_map/tri,tcj->rcij/transpose | solution.py:88
  1529.4 25.2 convolution_bitcast_fusion.1
  1554.6 44.3 %copy.371 = f32[4,8,1024,512]{3,2,1,0:T(8,128)} copy(f32[4,8,1024,512]{3,2,0,1:T(8,128)} %convolution_bitcast_fusion.1) | data formatting | bytes 134217728 | tf_op jit(solution)/shard_map/tci,trj->rcij/transpose | solution.py:95
  1598.9 42.3 copy.341
  1687.1 174.9 %reduce-scatter.23.cloned.1.call-done = f32[1,256,512]{2,1,0:T(8,128)} async-done(((f32[32,256,512]{2,1,0:T(8,128)}), f32[1,256,512]{2,1,0:T(8,128)}) %reduce-scatter.23.cloned.1.call-update) | async-done | bytes 524304 | tf_op jit(solution)/shard_map/reduce_scatter | solution.py:441
  1864.5 184.6 %reduce-scatter.17.cloned.1.call-done = f32[1,512,256]{2,1,0:T(8,128)} async-done(((f32[32,512,256]{2,1,0:T(8,128)}), f32[1,512,256]{2,1,0:T(8,128)}) %reduce-scatter.17.cloned.1.call-update) | async-done | bytes 524304 | tf_op jit(solution)/shard_map/reduce_scatter | solution.py:438
  2066.0 693.2 %reduce-scatter.27.cloned.1.call-done = f32[1,512,1024]{2,1,0:T(8,128)} async-done(((f32[32,512,1024]{2,1,0:T(8,128)}), f32[1,512,1024]{2,1,0:T(8,128)}) %reduce-scatter.27.cloned.1.call-update) | async-done | bytes 2097168 | tf_op jit(solution)/shard_map/reduce_scatter | solution.py:443
  2768.8 699.3 %reduce-scatter.25.cloned.1.call-done = f32[1,512,1024]{2,1,0:T(8,128)} async-done(((f32[32,512,1024]{2,1,0:T(8,128)}), f32[1,512,1024]{2,1,0:T(8,128)}) %reduce-scatter.25.cloned.1.call-update) | async-done | bytes 2097168 | tf_op jit(solution)/shard_map/reduce_scatter | solution.py:442
  3495.3 681.7 %reduce-scatter.29.cloned.1.call-done = f32[1,1024,512]{2,1,0:T(8,128)} async-done(((f32[32,1024,512]{2,1,0:T(8,128)}), f32[1,1024,512]{2,1,0:T(8,128)}) %reduce-scatter.29.cloned.1.call-update) | async-done | bytes 2097168 | tf_op jit(solution)/shard_map/reduce_scatter | solution.py:444
  (369 shorter events, 692.4 us)
Async XLA Ops:
  7.2 2752.0 %copy-start = (f32[1,512,512]{2,1,0:T(8,128)S(1)}, f32[1,512,512]{2,1,0:T(8,128)}, u32[]{:S(2)}) copy-start(f32[1,512,512]{2,1,0:T(8,128)} %param.83) | copy-start | bytes 3145732
  7.3 63.7 %all-gather.11.cloned.1.call-start = ((), (), s32[]{:S(2)}) async-start(), calls=%async_computation.10 | async-start | bytes 2162688 | tf_op jit(solution)/shard_map/all_gather | solution.py:271
  9.0 120.9 %all-gather.17.cloned.1.call-start = ((), (), s32[]{:S(2)}) async-start(), calls=%async_computation.13 | async-start | bytes 2162688 | tf_op jit(solution)/shard_map/all_gather | solution.py:272
  10.6 199.0 %all-gather.21.cloned.1.call-start = ((), (), s32[]{:S(2)}) async-start(), calls=%async_computation.15 | async-start | bytes 8650752 | tf_op jit(solution)/shard_map/all_gather | solution.py:273
  12.5 276.6 %all-gather.15.cloned.1.call-start = ((), (), s32[]{:S(2)}) async-start(), calls=%async_computation.12 | async-start | bytes 8650752 | tf_op jit(solution)/shard_map/all_gather | solution.py:270
  14.3 306.2 %all-gather.13.cloned.1.call-start = ((), (), s32[]{:S(2)}) async-start(), calls=%async_computation.11 | async-start | bytes 2359296 | tf_op jit(solution)/shard_map/all_gather | solution.py:337
  78.8 273.7 %all-gather.19.cloned.1.call-start = ((), (), s32[]{:S(2)}) async-start(), calls=%async_computation.14 | async-start | bytes 2359296 | tf_op jit(solution)/shard_map/all_gather | solution.py:338
  137.1 412.9 %all-gather.23.cloned.1.call-start = ((), (), s32[]{:S(2)}) async-start(), calls=%async_computation.16 | async-start | bytes 34603008 | tf_op jit(solution)/shard_map/all_gather | solution.py:274
  139.9 606.7 %all-gather.25.cloned.1.call-start = ((), (), s32[]{:S(2)}) async-start(), calls=%async_computation.17 | async-start | bytes 34603008 | tf_op jit(solution)/shard_map/all_gather | solution.py:275
  142.7 800.3 %all-gather.27.cloned.1.call-start = ((), (), s32[]{:S(2)}) async-start(), calls=%async_computation.18 | async-start | bytes 34603008 | tf_op jit(solution)/shard_map/all_gather | solution.py:276
  145.6 1062.3 %reduce-scatter.13.cloned.1.call-start = ((), (), s32[]{:S(2)}) async-start(), calls=%async_computation.19 | async-start | bytes 2359296 | tf_op jit(solution)/shard_map/reduce_scatter | solution.py:408
  383.8 446.7 %copy-start.18 = (bf16[256,2048]{1,0:T(8,128)(2,1)}, bf16[256,2048]{1,0:T(8,128)(2,1)S(1)}, u32[]{:S(2)}) copy-start(bf16[256,2048]{1,0:T(8,128)(2,1)S(1)} %multiply_convert_fusion.3) | copy-start | bytes 3145732
  1065.2 179.9 %reduce-scatter.15.cloned.1.call-start = ((), (), s32[]{:S(2)}) async-start(), calls=%async_computation.20 | async-start | bytes 2359296 | tf_op jit(solution)/shard_map/reduce_scatter | solution.py:411
  1069.1 595.2 %reduce-scatter.31.cloned.1.call-start = ((), (), s32[]{:S(2)}) async-start(), calls=%async_computation.28 | async-start | bytes 1081344
  1257.8 408.8 %reduce-scatter.19.cloned.1.call-start = ((), (), s32[]{:S(2)}) async-start(), calls=%async_computation.22 | async-start | bytes 4325376 | tf_op jit(solution)/shard_map/reduce_scatter | solution.py:439
  1266.1 409.5 %reduce-scatter.21.cloned.1.call-start = ((), (), s32[]{:S(2)}) async-start(), calls=%async_computation.23 | async-start | bytes 4325376 | tf_op jit(solution)/shard_map/reduce_scatter | solution.py:440
  1275.4 586.5 %reduce-scatter.23.cloned.1.call-start = ((), (), s32[]{:S(2)}) async-start(), calls=%async_computation.24 | async-start | bytes 17301504 | tf_op jit(solution)/shard_map/reduce_scatter | solution.py:441
  1303.2 746.0 %reduce-scatter.17.cloned.1.call-start = ((), (), s32[]{:S(2)}) async-start(), calls=%async_computation.21 | async-start | bytes 17301504 | tf_op jit(solution)/shard_map/reduce_scatter | solution.py:438
  1331.9 1427.2 %reduce-scatter.27.cloned.1.call-start = ((), (), s32[]{:S(2)}) async-start(), calls=%async_computation.26 | async-start | bytes 69206016 | tf_op jit(solution)/shard_map/reduce_scatter | solution.py:443
  1427.1 2040.9 %reduce-scatter.25.cloned.1.call-start = ((), (), s32[]{:S(2)}) async-start(), calls=%async_computation.25 | async-start | bytes 69206016 | tf_op jit(solution)/shard_map/reduce_scatter | solution.py:442
  1522.5 2654.5 %reduce-scatter.29.cloned.1.call-start = ((), (), s32[]{:S(2)}) async-start(), calls=%async_computation.27 | async-start | bytes 69206016 | tf_op jit(solution)/shard_map/reduce_scatter | solution.py:444
  1664.3 388.0 %copy-start.64 = (f32[1,256,256]{2,1,0:T(8,128)S(1)}, f32[1,256,256]{2,1,0:T(8,128)}, u32[]{:S(2)}) copy-start(f32[1,256,256]{2,1,0:T(8,128)} %param.73) | copy-start | bytes 786436
  2066.0 1410.9 %copy-start.27 = (f32[1,512,1024]{2,1,0:T(8,128)S(1)}, f32[1,512,1024]{2,1,0:T(8,128)}, u32[]{:S(2)}) copy-start(f32[1,512,1024]{2,1,0:T(8,128)} %param.80) | copy-start | bytes 6291460
  3495.3 698.0 %copy-start.29 = (f32[1,1024,512]{2,1,0:T(8,128)S(1)}, f32[1,1024,512]{2,1,0:T(8,128)}, u32[]{:S(2)}) copy-start(f32[1,1024,512]{2,1,0:T(8,128)} %param.85) | copy-start | bytes 6291460
  (80 other events, 3363.4 us)
Sparse Core Ops, SparseCore 0:
  11.6 59.2 all-gather.10
  74.5 55.3 all-gather.16
  133.5 76.1 all-gather.20
  213.0 75.9 all-gather.14
  291.1 29.4 all-gather.12
  322.6 29.8 all-gather.18
  356.1 193.8 all-gather.22
  553.5 192.9 all-gather.24
  750.1 192.9 all-gather.26
  1065.4 142.4 reduce-scatter.12
  1210.8 34.3 reduce-scatter.14
  1257.9 133.6 reduce-scatter.30
  1394.5 138.8 reduce-scatter.18
  1536.3 139.3 reduce-scatter.20
  1678.5 183.4 reduce-scatter.22
  1864.8 184.3 reduce-scatter.16
  2052.1 707.0 reduce-scatter.26
  2762.1 705.8 reduce-scatter.24
  3471.1 705.8 reduce-scatter.28
where the time goes:
time: 4260 us; the launch traced here: 4250 us
  waiting for transfers between devices  3220 us (76%)
  local copies, waits for them, and re-layouts  480 us (11%)
  matrix products  425 us (10%)
  other arithmetic  46.4 us (1%)
  blocking collectives  43 us (1%)
    reduce_scatter x1, waiting for transfers between devices, shards(): lax.psum_scatter(gate_grad, ('row', 'blk'), scatter_dimension=0, tiled=True)  699 us
    reduce_scatter x1, waiting for transfers between devices, shards(): lax.psum_scatter(up_grad, ('row', 'blk'), scatter_dimension=0, tiled=True)  693 us
    reduce_scatter x1, waiting for transfers between devices, shards(): lax.psum_scatter(down_grad, ('row', 'blk'), scatter_dimension=0, tiled=True)  682 us
    reshape x7, local copies, waits for them, and re-layouts, arrange(): return shard.reshape(row_parts, block_parts, shard.shape[1], shard.shape[2])  191 us
    reduce_scatter x1, waiting for transfers between devices, shards(): lax.psum_scatter(query_grad, ('row', 'blk'), scatter_dimension=0, tiled=T...  185 us
    reduce_scatter x1, waiting for transfers between devices, shards(): lax.psum_scatter(output_grad, ('row', 'blk'), scatter_dimension=0, tiled=...  175 us
    all_gather x1, waiting for transfers between devices, shards(): lax.all_gather(gate_weight.astype(jnp.bfloat16), ('row', 'blk'), axis=0,...  166 us
    transpose x3, local copies, waits for them, and re-layouts, block_grad(): jnp.einsum('tri,tcj->rcij', activations.reshape(token_count, row_parts, -...  143 us
  transfers between devices with their start and end apart: 19, of which 17 were waited for; matrix products, arithmetic and copies ran while one was open for 18% of the time, Pallas kernels for 0%

commit v1 on v0

v1 whole, which is shorter than its diff:
```python
import functools
import math

import jax
import jax.numpy as jnp
from jax import lax
from jax.experimental import pallas as pl
from jax.experimental.pallas import tpu as pltpu
from jax.sharding import PartitionSpec as P

HEADS = 32
KV_HEADS = 8
HEAD_DIM = 64
STEP = 10


NORM_EPSILON = 1e-05
ROPE_THETA = 500000.0
ROPE_FACTOR = 32.0
LOW_FACTOR = 1.0
HIGH_FACTOR = 4.0
BASE_SPAN = 8192.0
SCORE_SCALE = 0.125
MASKED = -1e30
SHAMPOO_DECAY = 0.95
SHAMPOO_RATE = 0.5
ADAM_RATE = 1.0
ADAM_FIRST = 0.9
ADAM_SECOND = 0.95
ADAM_EPSILON = 1e-08
QUERY_ROWS = 256
KEY_ROWS = 512
FEED_TILE = 512
BF16 = jnp.bfloat16
F32 = jnp.float32


def rope_rates():
    exponents = jnp.arange(0, HEAD_DIM, 2).astype(jnp.float32) / HEAD_DIM
    base_rates = 1.0 / ROPE_THETA**exponents
    wavelength = 2.0 * math.pi / base_rates
    smooth = (BASE_SPAN / wavelength - LOW_FACTOR) / (HIGH_FACTOR - LOW_FACTOR)
    blended = (1.0 - smooth) * base_rates / ROPE_FACTOR + smooth * base_rates
    longer = jnp.where(wavelength > BASE_SPAN / LOW_FACTOR, base_rates / ROPE_FACTOR, blended)
    return jnp.where(wavelength < BASE_SPAN / HIGH_FACTOR, base_rates, longer)


def adam_step(gradient, gains, first, second):
    first_new = ADAM_FIRST * first + (1.0 - ADAM_FIRST) * gradient
    second_new = ADAM_SECOND * second + (1.0 - ADAM_SECOND) * gradient * gradient
    corrected_first = first_new / (1.0 - ADAM_FIRST**STEP)
    corrected_second = second_new / (1.0 - ADAM_SECOND**STEP)
    return (
        first_new,
        second_new,
        gains - ADAM_RATE * corrected_first / (jnp.sqrt(corrected_second) + ADAM_EPSILON),
    )


def mul(left, right):
    return lax.dot_general(
        left, right, (((1,), (0,)), ((), ())), preferred_element_type=F32
    )


def mul_nt(left, right):
    return lax.dot_general(
        left, right, (((1,), (1,)), ((), ())), preferred_element_type=F32
    )


def mul_tn(left, right):
    return lax.dot_general(
        left, right, (((0,), (0,)), ((), ())), preferred_element_type=F32
    )


def turn(vectors, cos_table, sin_table):
    half = HEAD_DIM // 2
    former, latter = vectors[:half], vectors[half:]
    return jnp.concatenate(
        [former * cos_table - latter * sin_table, latter * cos_table + former * sin_table], axis=0
    )


def turn_back(vectors, cos_table, sin_table):
    return turn(vectors, cos_table, -sin_table)


def allowed_pairs(begins, query_block, key_block, query_rows, key_rows, copies):
    width = copies * query_rows
    key_index = key_block * key_rows + lax.broadcasted_iota(jnp.int32, (key_rows, width), 0)
    lane = lax.broadcasted_iota(jnp.int32, (1, query_rows), 1) + query_block * query_rows
    query_index = jnp.concatenate([lane] * copies, axis=1)
    begin_row = jnp.concatenate([begins] * copies, axis=1)
    return (key_index >= begin_row) & (key_index <= query_index)


def attend_kernel(
    copies,
    query_rows,
    key_rows,
    order_ref,
    first_ref,
    full_ref,
    begin_ref,
    qkv_ref,
    cos_ref,
    sin_ref,
    out_ref,
    query_ref,
    key_ref,
    keyt_ref,
    value_ref,
    lse_ref,
    valuet_ref,
):
    block = pl.program_id(0)
    width = copies * query_rows
    cos_table, sin_table = cos_ref[...], sin_ref[...]
    here = pl.ds(pl.multiple_of(block * query_rows, query_rows), query_rows)

    @pl.when(block == 0)
    def _():
        key_ref[...] = jnp.zeros_like(key_ref)
        keyt_ref[...] = jnp.zeros_like(keyt_ref)
        value_ref[...] = jnp.zeros_like(value_ref)
        valuet_ref[...] = jnp.zeros_like(valuet_ref)

    base = copies * HEAD_DIM
    keys = turn(qkv_ref[base : base + HEAD_DIM, :], cos_table, sin_table)
    values = qkv_ref[base + HEAD_DIM : base + 2 * HEAD_DIM, :]
    keyt_ref[:, here] = keys.astype(BF16)
    valuet_ref[:, here] = values.astype(BF16)
    key_ref[here, :] = keys.T.astype(BF16)
    value_ref[here, :] = values.T.astype(BF16)
    queries = jnp.concatenate(
        [
            turn(qkv_ref[h * HEAD_DIM : (h + 1) * HEAD_DIM, :], cos_table, sin_table)
            for h in range(copies)
        ],
        axis=1,
    ).astype(BF16) * jnp.asarray(SCORE_SCALE, BF16)
    query_ref[0] = queries
    begins = begin_ref[0]

    def visit(masked, number, state):
        peaks, totals, sums = state
        there = pl.ds(pl.multiple_of(number * key_rows, key_rows), key_rows)
        scores = mul(key_ref[there, :], queries)
        if masked:
            scores = jnp.where(
                allowed_pairs(begins, block, number, query_rows, key_rows, copies), scores, MASKED
            )
        new_peaks = jnp.maximum(peaks, jnp.max(scores, axis=0, keepdims=True))
        weights = jnp.exp(scores - new_peaks)
        factor = jnp.exp(peaks - new_peaks)
        totals = totals * factor + jnp.sum(weights, axis=0, keepdims=True)
        sums = sums * factor + mul(valuet_ref[:, there], weights.astype(BF16))
        return (new_peaks, totals, sums)

    state = (
        jnp.full((1, width), MASKED, F32),
        jnp.zeros((1, width), F32),
        jnp.zeros((HEAD_DIM, width), F32),
    )
    last = (block * query_rows) // key_rows
    first, full = first_ref[block], full_ref[block]
    state = lax.fori_loop(first, full, functools.partial(visit, True), state)
    state = lax.fori_loop(full, last, functools.partial(visit, False), state)
    peaks, totals, sums = visit(True, last, state)
    outs = (sums / totals).astype(BF16)
    for h in range(copies):
        out_ref[h * HEAD_DIM : (h + 1) * HEAD_DIM, :] = outs[:, h * query_rows : (h + 1) * query_rows]
    lse_ref[0] = peaks + jnp.log(totals)


def attend_back_kernel(
    copies,
    query_rows,
    key_rows,
    order_ref,
    first_ref,
    full_ref,
    begin_ref,
    query_ref,
    key_ref,
    keyt_ref,
    value_ref,
    lse_ref,
    out_ref,
    grad_ref,
    cos_ref,
    sin_ref,
    result_ref,
    dkey_ref,
    dvalue_ref,
):
    block = pl.program_id(0)
    width = copies * query_rows
    here = pl.ds(pl.multiple_of(block * query_rows, query_rows), query_rows)

    @pl.when(block == 0)
    def _():
        dkey_ref[...] = jnp.zeros_like(dkey_ref)
        dvalue_ref[...] = jnp.zeros_like(dvalue_ref)

    def place(number):
        return pl.ds(pl.multiple_of(order_ref[number] * query_rows, query_rows), query_rows)

    def spread(ref):
        return jnp.concatenate(
            [ref[h * HEAD_DIM : (h + 1) * HEAD_DIM, :] for h in range(copies)], axis=1
        )

    queries = query_ref[0]
    grads = spread(grad_ref)
    deltas = jnp.sum(grads.astype(F32) * spread(out_ref).astype(F32), axis=0, keepdims=True)
    lse = lse_ref[0]
    begins = begin_ref[0]

    def visit(masked, number, dquery):
        there = pl.ds(pl.multiple_of(number * key_rows, key_rows), key_rows)
        weights = jnp.exp(mul(key_ref[there, :], queries) - lse)
        if masked:
            weights = jnp.where(
                allowed_pairs(begins, block, number, query_rows, key_rows, copies), weights, 0.0
            )
        weight_grads = mul(value_ref[there, :], grads)
        score_grads = (weights * (weight_grads - deltas)).astype(BF16)
        dvalue_ref[there, :] += mul_nt(weights.astype(BF16), grads)
        dkey_ref[there, :] += mul_nt(score_grads, queries)
        return dquery + mul(keyt_ref[:, there], score_grads)

    last = (block * query_rows) // key_rows
    first, full = first_ref[block], full_ref[block]
    dquery = jnp.zeros((HEAD_DIM, width), F32)
    dquery = lax.fori_loop(first, full, functools.partial(visit, True), dquery)
    dquery = lax.fori_loop(full, last, functools.partial(visit, False), dquery)
    dquery = visit(True, last, dquery) * SCORE_SCALE
    cos_table, sin_table = cos_ref[:, here], sin_ref[:, here]
    for h in range(copies):
        piece = turn_back(dquery[:, h * query_rows : (h + 1) * query_rows], cos_table, sin_table)
        result_ref[h * HEAD_DIM : (h + 1) * HEAD_DIM, place(block)] = piece.astype(BF16)

    @pl.when(block == pl.num_programs(0) - 1)
    def _():
        base = copies * HEAD_DIM

        def finish(number, carried):
            rows = pl.ds(pl.multiple_of(number * query_rows, query_rows), query_rows)
            there = place(number)
            dkeys = turn_back(dkey_ref[rows, :].T, cos_ref[:, rows], sin_ref[:, rows])
            result_ref[base : base + HEAD_DIM, there] = dkeys.astype(BF16)
            dvalues = dvalue_ref[rows, :].T.astype(BF16)
            result_ref[base + HEAD_DIM : base + 2 * HEAD_DIM, there] = dvalues
            return carried

        lax.fori_loop(0, pl.num_programs(0), finish, 0)


def attend(qkv, cos_table, sin_table, begins, order, first, full, copies, query_rows, key_rows):
    total = qkv.shape[1]
    blocks = total // query_rows
    base = copies * HEAD_DIM
    width = copies * query_rows
    pairs = copies * total * total // 2
    return pl.pallas_call(
        functools.partial(attend_kernel, copies, query_rows, key_rows),
        grid_spec=pltpu.PrefetchScalarGridSpec(
        num_scalar_prefetch=3,
        grid=(blocks,),
        in_specs=[
            pl.BlockSpec((1, 1, query_rows), lambda i, order, first, full: (i, 0, 0)),
            pl.BlockSpec((base + 2 * HEAD_DIM, query_rows), lambda i, order, first, full: (0, order[i])),
            pl.BlockSpec((HEAD_DIM // 2, query_rows), lambda i, order, first, full: (0, i)),
            pl.BlockSpec((HEAD_DIM // 2, query_rows), lambda i, order, first, full: (0, i)),
        ],
        out_specs=[
            pl.BlockSpec((base, query_rows), lambda i, order, first, full: (0, order[i])),
            pl.BlockSpec((1, HEAD_DIM, width), lambda i, order, first, full: (i, 0, 0)),
            pl.BlockSpec((total, HEAD_DIM), lambda i, order, first, full: (0, 0)),
            pl.BlockSpec((HEAD_DIM, total), lambda i, order, first, full: (0, 0)),
            pl.BlockSpec((total, HEAD_DIM), lambda i, order, first, full: (0, 0)),
            pl.BlockSpec((1, 1, width), lambda i, order, first, full: (i, 0, 0)),
        ],
        scratch_shapes=[pltpu.VMEM((HEAD_DIM, total), BF16)],
        ),
        out_shape=[
            jax.ShapeDtypeStruct((base, total), BF16),
            jax.ShapeDtypeStruct((blocks, HEAD_DIM, width), BF16),
            jax.ShapeDtypeStruct((total, HEAD_DIM), BF16),
            jax.ShapeDtypeStruct((HEAD_DIM, total), BF16),
            jax.ShapeDtypeStruct((total, HEAD_DIM), BF16),
            jax.ShapeDtypeStruct((blocks, 1, width), F32),
        ],
        compiler_params=pltpu.CompilerParams(
            dimension_semantics=("arbitrary",), vmem_limit_bytes=48 * 1024 * 1024
        ),
        cost_estimate=pl.CostEstimate(
            flops=4 * pairs * HEAD_DIM, bytes_accessed=8 * 1024 * 1024, transcendentals=pairs
        ),
        name="attend",
    )(order, first, full, begins, qkv, cos_table, sin_table)


def attend_back(
    saved, grads, cos_table, sin_table, begins, order, first, full, copies, query_rows, key_rows
):
    out, queries, keys, keys_t, values, lse = saved
    total = keys.shape[0]
    blocks = total // query_rows
    base = copies * HEAD_DIM
    width = copies * query_rows
    pairs = copies * total * total // 2
    whole = lambda i, order, first, full: (0, 0)
    return pl.pallas_call(
        functools.partial(attend_back_kernel, copies, query_rows, key_rows),
        grid_spec=pltpu.PrefetchScalarGridSpec(
        num_scalar_prefetch=3,
        grid=(blocks,),
        in_specs=[
            pl.BlockSpec((1, 1, query_rows), lambda i, order, first, full: (i, 0, 0)),
            pl.BlockSpec((1, HEAD_DIM, width), lambda i, order, first, full: (i, 0, 0)),
            pl.BlockSpec((total, HEAD_DIM), whole),
            pl.BlockSpec((HEAD_DIM, total), whole),
            pl.BlockSpec((total, HEAD_DIM), whole),
            pl.BlockSpec((1, 1, width), lambda i, order, first, full: (i, 0, 0)),
            pl.BlockSpec((base, query_rows), lambda i, order, first, full: (0, order[i])),
            pl.BlockSpec((base, query_rows), lambda i, order, first, full: (0, order[i])),
            pl.BlockSpec((HEAD_DIM // 2, total), whole),
            pl.BlockSpec((HEAD_DIM // 2, total), whole),
        ],
        out_specs=pl.BlockSpec((base + 2 * HEAD_DIM, total), whole),
        scratch_shapes=[
            pltpu.VMEM((total, HEAD_DIM), F32),
            pltpu.VMEM((total, HEAD_DIM), F32),
        ],
        ),
        out_shape=jax.ShapeDtypeStruct((base + 2 * HEAD_DIM, total), BF16),
        compiler_params=pltpu.CompilerParams(
            dimension_semantics=("arbitrary",), vmem_limit_bytes=48 * 1024 * 1024
        ),
        cost_estimate=pl.CostEstimate(
            flops=10 * pairs * HEAD_DIM, bytes_accessed=8 * 1024 * 1024, transcendentals=pairs
        ),
        name="attend_back",
    )(
        order, first, full, begins, queries, keys, keys_t, values, lse, out, grads, cos_table, sin_table
    )


def norm(rows):
    inverse = lax.rsqrt(jnp.mean(rows * rows, axis=-1, keepdims=True) + NORM_EPSILON)
    return rows * inverse, inverse


def norm_back(gradient, normed, inverse):
    return inverse * (gradient - normed * jnp.mean(gradient * normed, axis=-1, keepdims=True))


def project_kernel(gains_ref, weight_ref, own_ref, other_ref, *refs):
    scaled_ref, result_ref = refs[-2:]
    rows = own_ref.shape[0]
    for half, ref in enumerate((own_ref, other_ref)):
        chunk = ref[...].astype(F32)
        inverse = lax.rsqrt(jnp.mean(chunk * chunk, axis=-1, keepdims=True) + NORM_EPSILON)
        scaled = (chunk * inverse * gains_ref[...]).astype(BF16)
        scaled_ref[0, half * rows : (half + 1) * rows, :] = scaled
        result_ref[:, half * rows : (half + 1) * rows] = mul_nt(weight_ref[...], scaled)


def project(step, places, gains, weight, own, other, held):
    rows, width = own.shape
    outputs = weight.shape[0]
    whole = lambda i: (0, 0)
    return pl.pallas_call(
        project_kernel,
        grid=(1,),
        in_specs=[
            pl.BlockSpec((1, width), whole),
            pl.BlockSpec((outputs, width), whole),
            pl.BlockSpec((rows, width), whole),
            pl.BlockSpec((rows, width), whole),
        ]
        + [pl.BlockSpec(memory_space=pl.ANY)] * len(held),
        out_specs=[
            pl.BlockSpec((1, 2 * rows, width), lambda i: (step, 0, 0)),
            pl.BlockSpec((outputs, 2 * rows), lambda i: (0, step)),
        ],
        out_shape=[
            jax.ShapeDtypeStruct((places, 2 * rows, width), BF16),
            jax.ShapeDtypeStruct((outputs, places * 2 * rows), F32),
        ],
        input_output_aliases={4 + n: n for n in range(len(held))},
        compiler_params=pltpu.CompilerParams(vmem_limit_bytes=48 * 1024 * 1024),
        cost_estimate=pl.CostEstimate(
            flops=4 * rows * width * outputs, bytes_accessed=8 * rows * width, transcendentals=0
        ),
        name="project",
    )(gains, weight, own, other, *held)


def feed_kernel(
    row_parts, where_ref, own_ref, other_ref, grad_own_ref, grad_other_ref, *refs
):
    gate_refs, up_refs, down_refs = [
        refs[n * row_parts : (n + 1) * row_parts] for n in range(3)
    ]
    (
        scaled_ref,
        upstream_ref,
        hidden_ref,
        gate_low_ref,
        up_low_ref,
        back_own_ref,
        back_other_ref,
        out_own_ref,
        out_other_ref,
        back_ref,
        out_ref,
    ) = refs[-11:]
    step = pl.program_id(0)
    rows = own_ref.shape[0]
    size = down_refs[0].shape[1]

    @pl.when(step == 0)
    def _():
        scaled_ref[0, :rows, :] = own_ref[...]
        scaled_ref[0, rows:, :] = other_ref[...]
        upstream_ref[0, :rows, :] = grad_own_ref[...]
        upstream_ref[0, rows:, :] = grad_other_ref[...]
        out_ref[...] = jnp.zeros_like(out_ref)
        back_ref[...] = jnp.zeros_like(back_ref)

    places = [
        pl.ds(pl.multiple_of(where_ref[part] * size, size), size) for part in range(row_parts)
    ]
    gate_pre = up_pre = hidden_grad = 0.0
    for part, here in enumerate(places):
        scaled = scaled_ref[0, :, here]
        gate_pre += mul(scaled, gate_refs[part][...])
        up_pre += mul(scaled, up_refs[part][...])
        hidden_grad += mul_nt(upstream_ref[0, :, here], down_refs[part][...])
    sigmoid_gate = 1.0 / (1.0 + jnp.exp(-gate_pre))
    silu_gate = gate_pre * sigmoid_gate
    hidden = (silu_gate * up_pre).astype(BF16)
    gate_low = (hidden_grad * up_pre * sigmoid_gate * (1.0 + gate_pre * (1.0 - sigmoid_gate))).astype(
        BF16
    )
    up_low = (hidden_grad * silu_gate).astype(BF16)
    hidden_ref[0] = hidden
    gate_low_ref[0] = gate_low
    up_low_ref[0] = up_low
    both_low = jnp.concatenate([gate_low, up_low], axis=1)
    for part, here in enumerate(places):
        out_ref[:, here] += mul(hidden, down_refs[part][...])
        both = jnp.concatenate([gate_refs[part][...], up_refs[part][...]], axis=1)
        back_ref[:, here] += mul_nt(both_low, both)

    @pl.when(step == pl.num_programs(0) - 1)
    def _():
        back_own_ref[...] = back_ref[:rows, :].astype(BF16)
        back_other_ref[...] = back_ref[rows:, :].astype(BF16)
        out_own_ref[...] = out_ref[:rows, :].astype(BF16)
        out_other_ref[...] = out_ref[rows:, :].astype(BF16)


def feed(step, places, where, own, other, grad_own, grad_other, weights, held):
    rows, width = own.shape
    row_parts = len(weights[0])
    size, inner = weights[1][0].shape
    tile = min(FEED_TILE, inner, size)
    tall = size // tile
    shard = pl.BlockSpec((rows, width), lambda i, where: (0, 0))
    gate = pl.BlockSpec((size, tile), lambda i, where: (0, i))
    down = pl.BlockSpec((tile, size), lambda i, where: (i % tall, i // tall))
    kept = pl.BlockSpec((1, 2 * rows, width), lambda i, where: (step, 0, 0))
    kept_inner = pl.BlockSpec((1, 2 * rows, tile), lambda i, where: (step, 0, i))
    return pl.pallas_call(
        functools.partial(feed_kernel, row_parts),
        grid_spec=pltpu.PrefetchScalarGridSpec(
            num_scalar_prefetch=1,
            grid=(inner // tile,),
            in_specs=[shard] * 4
            + [gate] * (2 * row_parts)
            + [down] * row_parts
            + [pl.BlockSpec(memory_space=pl.ANY)] * len(held),
            out_specs=[kept] * 2
            + [kept_inner] * 3
            + [shard] * 4,
            scratch_shapes=[pltpu.VMEM((2 * rows, width), F32)] * 2,
        ),
        out_shape=[jax.ShapeDtypeStruct((places, 2 * rows, width), BF16)] * 2
        + [jax.ShapeDtypeStruct((places, 2 * rows, inner), BF16)] * 3
        + [jax.ShapeDtypeStruct((rows, width), BF16)] * 4,
        input_output_aliases={5 + 3 * row_parts + n: n for n in range(len(held))},
        compiler_params=pltpu.CompilerParams(
            dimension_semantics=("arbitrary",), vmem_limit_bytes=60 * 1024 * 1024
        ),
        cost_estimate=pl.CostEstimate(
            flops=24 * rows * width * inner,
            bytes_accessed=32 * rows * width + 6 * width * inner,
            transcendentals=2 * rows * inner,
        ),
        name="feed",
    )(
        where, own, other, grad_own, grad_other, *weights[0], *weights[1], *weights[2], *held
    )


def split_kernel(base, where_ref, entry_ref, send_ref):
    blocks, rows, _ = send_ref.shape
    key_in = rows - 16
    key_out = entry_ref.shape[2] - base
    per_row = key_out // HEAD_DIM
    shares = blocks // KV_HEADS
    line = lax.broadcasted_iota(jnp.int32, (16, 2 * HEAD_DIM), 0)
    gains = jnp.zeros((16, 2 * HEAD_DIM), F32)
    for part in range(entry_ref.shape[0]):
        here = where_ref[part]
        top = entry_ref[here, 2 * key_in : 2 * key_in + 16, : 2 * HEAD_DIM].astype(F32)
        gains = jnp.where(line == part, top[:1], gains)
    for head in range(KV_HEADS):
        here = where_ref[head // per_row]
        start = base + head % per_row * HEAD_DIM
        piece = jnp.concatenate(
            [
                entry_ref[here, :key_in, start : start + HEAD_DIM],
                entry_ref[here, key_in : 2 * key_in, start : start + HEAD_DIM],
            ],
            axis=1,
        )
        for number in range(head * shares, (head + 1) * shares):
            send_ref[number, :key_in, :] = piece
            send_ref[number, key_in:, :] = gains.astype(BF16)


def split_entry(where, entry, base, blocks, key_in):
    return pl.pallas_call(
        functools.partial(split_kernel, base),
        grid_spec=pltpu.PrefetchScalarGridSpec(
            num_scalar_prefetch=1,
            grid=(1,),
            in_specs=[pl.BlockSpec(entry.shape, lambda i, where: (0, 0, 0))],
            out_specs=pl.BlockSpec(
                (blocks, key_in + 16, 2 * HEAD_DIM), lambda i, where: (0, 0, 0)
            ),
        ),
        out_shape=jax.ShapeDtypeStruct((blocks, key_in + 16, 2 * HEAD_DIM), BF16),
        name="split_entry",
    )(where, entry)


def join_kernel(base, where_ref, entry_ref, kv_ref, plain_ref, turned_ref):
    blocks, rows, depth = kv_ref.shape
    key_in = rows - 16
    size = entry_ref.shape[1] - 16
    for part in range(entry_ref.shape[0]):
        block = entry_ref[where_ref[part], :size, :base]
        here = slice(part * size, (part + 1) * size)
        plain_ref[here, :base] = block
        turned_ref[:base, here] = block.astype(F32).T.astype(BF16)
    for number in range(blocks):
        block = kv_ref[number, :key_in, :]
        here = slice(number * key_in, (number + 1) * key_in)
        plain_ref[here, base:] = block
        turned_ref[base:, here] = block.astype(F32).T.astype(BF16)


def join_weights(where, entry, kv, base, width):
    depth = base + 2 * HEAD_DIM
    return pl.pallas_call(
        functools.partial(join_kernel, base),
        grid_spec=pltpu.PrefetchScalarGridSpec(
            num_scalar_prefetch=1,
            grid=(1,),
            in_specs=[
                pl.BlockSpec(entry.shape, lambda i, where: (0, 0, 0)),
                pl.BlockSpec(kv.shape, lambda i, where: (0, 0, 0)),
            ],
            out_specs=[
                pl.BlockSpec((width, depth), lambda i, where: (0, 0)),
                pl.BlockSpec((depth, width), lambda i, where: (0, 0)),
            ],
        ),
        out_shape=[
            jax.ShapeDtypeStruct((width, depth), BF16),
            jax.ShapeDtypeStruct((depth, width), BF16),
        ],
        name="join_weights",
    )(where, entry, kv)


def projection_grad_kernel(base, grads_ref, scaled_ref, weight_ref, query_ref, kv_ref, gain_ref):
    product = mul(grads_ref[...], scaled_ref[...])
    gain_ref[...] = jnp.sum(product * weight_ref[...].astype(F32), axis=0, keepdims=True)
    query_ref[0] = product[:base].T.astype(BF16)
    count, size, _ = kv_ref.shape
    for number in range(count):
        kv_ref[number] = product[base:, number * size : (number + 1) * size].T.astype(BF16)


def projection_grad(grads, scaled, weight, base, row_parts, block_parts):
    depth, total = grads.shape
    width = scaled.shape[1]
    size, key_in = width // row_parts, width // block_parts
    count = block_parts // row_parts
    return pl.pallas_call(
        functools.partial(projection_grad_kernel, base),
        grid=(row_parts,),
        in_specs=[
            pl.BlockSpec((depth, total), lambda i: (0, 0)),
            pl.BlockSpec((total, size), lambda i: (0, i)),
            pl.BlockSpec((depth, size), lambda i: (0, i)),
        ],
        out_specs=[
            pl.BlockSpec((1, size, base), lambda i: (i, 0, 0)),
            pl.BlockSpec((count, key_in, depth - base), lambda i: (i, 0, 0)),
            pl.BlockSpec((1, size), lambda i: (0, i)),
        ],
        out_shape=[
            jax.ShapeDtypeStruct((row_parts, size, base), BF16),
            jax.ShapeDtypeStruct((block_parts, key_in, depth - base), BF16),
            jax.ShapeDtypeStruct((1, width), F32),
        ],
        compiler_params=pltpu.CompilerParams(
            dimension_semantics=("arbitrary",), vmem_limit_bytes=48 * 1024 * 1024
        ),
        cost_estimate=pl.CostEstimate(
            flops=2 * depth * total * width, bytes_accessed=2 * total * width, transcendentals=0
        ),
        name="projection_grad",
    )(grads, scaled, weight)


def shampoo_kernel(
    gradient_ref,
    columns_ref,
    master_ref,
    left_ref,
    right_ref,
    left_root_ref,
    right_root_ref,
    wide_ref,
    new_ref,
    left_new_ref,
    right_new_ref,
):
    rows = master_ref.shape[1]
    here = pl.ds(pl.multiple_of(pl.program_id(0) * rows, rows), rows)
    gradient = gradient_ref[...].astype(BF16)
    mine = gradient_ref[here, :].astype(F32)
    wide_ref[0] = mine
    left = mul_nt(mine.astype(BF16), gradient)
    left_new_ref[0] = SHAMPOO_DECAY * left_ref[0] + (1.0 - SHAMPOO_DECAY) * left
    turned = columns_ref[...].astype(F32).T.astype(BF16)
    right = mul(turned, gradient)
    right_new_ref[0] = SHAMPOO_DECAY * right_ref[0] + (1.0 - SHAMPOO_DECAY) * right
    half = mul(left_root_ref[0].astype(BF16), gradient).astype(BF16)
    direction = mul(half, right_root_ref[0].astype(BF16))
    new_ref[0] = master_ref[0] - SHAMPOO_RATE * direction


def shampoo(gradient, master, left, right, left_root, right_root):
    rows, columns = gradient.shape
    steps = max(1, min(4, columns // 128))
    tile, wide = rows // steps, columns // steps

    def lines(height, width):
        return pl.BlockSpec((1, height, width), lambda i: (0, i, 0))

    return pl.pallas_call(
        shampoo_kernel,
        grid=(steps,),
        in_specs=[
            pl.BlockSpec((rows, columns), lambda i: (0, 0)),
            pl.BlockSpec((rows, wide), lambda i: (0, i)),
            lines(tile, columns),
            lines(tile, rows),
            lines(wide, columns),
            lines(tile, rows),
            pl.BlockSpec((1, columns, columns), lambda i: (0, 0, 0)),
        ],
        out_specs=[lines(tile, columns)] * 2 + [lines(tile, rows), lines(wide, columns)],
        out_shape=[jax.ShapeDtypeStruct(master.shape, F32)] * 2
        + [jax.ShapeDtypeStruct(left.shape, F32), jax.ShapeDtypeStruct(right.shape, F32)],
        compiler_params=pltpu.CompilerParams(
            dimension_semantics=("arbitrary",), vmem_limit_bytes=48 * 1024 * 1024
        ),
        cost_estimate=pl.CostEstimate(
            flops=4 * rows * columns * (rows + columns),
            bytes_accessed=12 * (rows * rows + columns * columns + rows * columns),
            transcendentals=0,
        ),
        name="shampoo",
    )(gradient, gradient, master, left, right, left_root, right_root)


def arrange_kernel(width, where_ref, *refs):
    result_ref = refs[-1]
    count, wide = refs[0].shape
    for part, ref in enumerate(refs[:-1]):
        here = pl.ds(pl.multiple_of(where_ref[part] * width, width), width)
        for piece in range(wide // width):
            rows = slice(piece * count, (piece + 1) * count)
            result_ref[rows, here] = ref[:, piece * width : (piece + 1) * width]


def arrange_output(where, items, start, base, width):
    count = items[0].shape[0] - start
    wide = items[0].shape[1]
    row_parts = len(items)
    return pl.pallas_call(
        functools.partial(arrange_kernel, width // row_parts),
        grid_spec=pltpu.PrefetchScalarGridSpec(
            num_scalar_prefetch=1,
            grid=(1,),
            in_specs=[
                pl.BlockSpec((count, wide), lambda i, where: (start // count, 0))
            ]
            * row_parts,
            out_specs=pl.BlockSpec((base, width), lambda i, where: (0, 0)),
        ),
        out_shape=jax.ShapeDtypeStruct((base, width), BF16),
        name="arrange_output",
    )(where, *items)


def down_grad_kernel(hidden_ref, upstream_ref, result_ref, turned_ref):
    rows = 256

    @pl.when(pl.program_id(0) == 0)
    def _():
        def turn_rows(number, carried):
            here = pl.ds(pl.multiple_of(number * rows, rows), rows)
            turned_ref[:, here] = hidden_ref[here, :].astype(F32).T.astype(BF16)
            return carried

        lax.fori_loop(0, hidden_ref.shape[0] // rows, turn_rows, 0)

    result_ref[0] = mul(turned_ref[...], upstream_ref[...]).astype(BF16)


def down_gradient(hidden, upstream, row_parts):
    total, inner = hidden.shape
    width = upstream.shape[1]
    size = width // row_parts
    return pl.pallas_call(
        down_grad_kernel,
        grid=(row_parts,),
        in_specs=[
            pl.BlockSpec((total, inner), lambda i: (0, 0)),
            pl.BlockSpec((total, size), lambda i: (0, i)),
        ],
        out_specs=pl.BlockSpec((1, inner, size), lambda i: (i, 0, 0)),
        out_shape=jax.ShapeDtypeStruct((row_parts, inner, size), BF16),
        scratch_shapes=[pltpu.VMEM((inner, total), BF16)],
        compiler_params=pltpu.CompilerParams(
            dimension_semantics=("arbitrary",), vmem_limit_bytes=48 * 1024 * 1024
        ),
        cost_estimate=pl.CostEstimate(
            flops=2 * total * inner * width,
            bytes_accessed=2 * total * (inner + width),
            transcendentals=0,
        ),
        name="down_gradient",
    )(hidden, upstream)


def spread_kernel(rows_ref, weight_ref, *out_refs):
    block = pl.program_id(0)
    part = mul(rows_ref[...].astype(F32).T.astype(BF16), weight_ref[...]).astype(BF16)
    for number, ref in enumerate(out_refs):

        @pl.when(block == number)
        def _():
            ref[...] = part


def spread_parts(rows, weight, blocks):
    depth, total = rows.shape
    width = weight.shape[1]
    count = total // blocks
    shard = pl.BlockSpec((count, width), lambda i: (0, 0))
    return pl.pallas_call(
        spread_kernel,
        grid=(blocks,),
        in_specs=[
            pl.BlockSpec((depth, count), lambda i: (0, i)),
            pl.BlockSpec((depth, width), lambda i: (0, 0)),
        ],
        out_specs=[shard] * blocks,
        out_shape=[jax.ShapeDtypeStruct((count, width), BF16)] * blocks,
        compiler_params=pltpu.CompilerParams(
            dimension_semantics=("arbitrary",), vmem_limit_bytes=48 * 1024 * 1024
        ),
        cost_estimate=pl.CostEstimate(
            flops=2 * depth * total * width,
            bytes_accessed=2 * total * width,
            transcendentals=0,
        ),
        name="spread",
    )(rows, weight)


def output_back_kernel(columns, weight_ref, attended_ref, *refs):
    shard_refs, out_grad_ref, weight_grad_ref = refs[:-2], refs[-2], refs[-1]
    count = shard_refs[0].shape[0]
    total = None
    for number, ref in enumerate(shard_refs):
        shard = ref[...]
        here = slice(number * count, (number + 1) * count)
        out_grad_ref[:, here] = mul_nt(weight_ref[...], shard).astype(BF16)
        part = mul(attended_ref[:, here], shard)
        total = part if total is None else total + part
    for piece in range(weight_grad_ref.shape[0]):
        weight_grad_ref[piece] = total[:, piece * columns : (piece + 1) * columns].astype(BF16)


def output_back(weight, attended, shards_all, row_parts):
    depth, width = weight.shape
    total = attended.shape[1]
    columns = width // row_parts
    whole = lambda i: (0, 0)
    return pl.pallas_call(
        functools.partial(output_back_kernel, columns),
        grid=(1,),
        in_specs=[pl.BlockSpec((depth, width), whole), pl.BlockSpec((depth, total), whole)]
        + [pl.BlockSpec(item.shape, whole) for item in shards_all],
        out_specs=[
            pl.BlockSpec((depth, total), whole),
            pl.BlockSpec((row_parts, depth, columns), lambda i: (0, 0, 0)),
        ],
        out_shape=[
            jax.ShapeDtypeStruct((depth, total), BF16),
            jax.ShapeDtypeStruct((row_parts, depth, columns), BF16),
        ],
        compiler_params=pltpu.CompilerParams(vmem_limit_bytes=52 * 1024 * 1024),
        cost_estimate=pl.CostEstimate(
            flops=4 * depth * total * width, bytes_accessed=2 * total * width, transcendentals=0
        ),
        name="output_back",
    )(weight, attended, *shards_all)


def together(*values):
    return lax.optimization_barrier(values)


def after(value, *others):
    return lax.optimization_barrier((value,) + others)[0]


def send(array, pairs):
    both = [(2 * here + core, 2 * there + core) for here, there in pairs for core in range(2)]
    return lax.ppermute(array, "blk", both)


def row_send(array, row_parts, flip):
    return lax.ppermute(array, "row", [(n, n ^ flip) for n in range(row_parts)])


def row_sends(block, row_parts, flips=None):
    return [row_send(block, row_parts, flip) for flip in (flips or range(1, row_parts))]


def row_exchange(pieces):
    me = lax.axis_index("row")
    items = [
        lax.dynamic_index_in_dim(pieces, me ^ flip, 0, False) for flip in range(len(pieces))
    ]
    return [items[0]] + [row_send(items[n], len(items), n) for n in range(1, len(items))]


def row_sum(items):
    return sum(item.astype(F32) for item in items)


def shards(*arguments):
    (inputs, cotangent, doc_lengths, norm_gains, gain_first, gain_second) = arguments[:6]
    state = [arguments[6 + 5 * n : 11 + 5 * n] for n in range(7)]
    query_weight, key_weight, value_weight, output_weight, gate_weight, up_weight, down_weight = [
        group[0][0] for group in state
    ]
    row_parts = lax.axis_size("row")
    block_parts = lax.axis_size("blk")
    devices = row_parts * block_parts
    places = block_parts // 2
    copies = HEADS // block_parts
    shares = block_parts // KV_HEADS
    token_count = inputs.shape[1]
    total = token_count * block_parts
    width = inputs.shape[2]
    base = copies * HEAD_DIM
    gain_width = norm_gains.shape[1]
    key_in, key_out = key_weight.shape
    query_in = query_weight.shape[0]
    inner = gate_weight.shape[1]
    me = lax.axis_index("blk")
    place = me // 2
    upward = [(n, (n + 1) % places) for n in range(places)]
    downward = [(n, (n - 1) % places) for n in range(places)]
    head_pair = 2 * HEAD_DIM
    spare = 16

    def low(array):
        return array.astype(BF16)

    def pad_to(array, rows, columns):
        return jnp.pad(array, ((0, rows - array.shape[0]), (0, columns - array.shape[1])))

    def swapped(array):
        return lax.ppermute(array, "blk", [(n, n ^ 1) for n in range(block_parts)])

    where = lax.axis_index("row") ^ jnp.arange(row_parts, dtype=jnp.int32)
    down_wide = down_weight.reshape(inner // query_in, query_in, query_in).transpose(1, 0, 2)
    down_wide = down_wide.reshape(query_in, inner)
    half_flips = list(range(1, row_parts - 1)), [row_parts - 1]

    shard = inputs[0]
    entry = jnp.concatenate([low(query_weight), low(jnp.concatenate([key_weight, value_weight]))], 1)
    gain_line = low(norm_gains).reshape(1, 2 * gain_width)
    entry = jnp.concatenate([entry, pad_to(gain_line, spare, entry.shape[1])], axis=0)
    tokens = [shard, send(shard, upward)]
    pieces = inner // output_weight.shape[1]
    output_wide = jnp.concatenate(jnp.split(low(output_weight), pieces, axis=0), axis=1)
    tokens[1], gate_low, *entries = together(
        tokens[1],
        jnp.concatenate([low(gate_weight), output_wide], axis=0),
        *row_sends(entry, row_parts),
    )
    entry = jnp.stack([entry, *entries])
    kv_send = split_entry(where, entry, base, block_parts, key_in)
    token_others = [swapped(shard)]
    following = send(tokens[1], upward)
    following, kv_slice, entry, down_low, up_low_weight, *gate_items = together(
        following,
        lax.all_to_all(kv_send, "blk", 0, 0),
        entry,
        low(down_wide),
        low(up_weight),
        *row_sends(gate_low, row_parts, half_flips[0]),
    )
    tokens.append(following)
    qkv_full, qkv_turned = join_weights(where, entry, kv_slice, base, width)
    gains = kv_slice[:, key_in : key_in + row_parts, : 2 * gain_width]
    gains = gains.reshape(block_parts, row_parts, 2, gain_width).transpose(2, 1, 0, 3)
    gains = gains.reshape(2, 1, width).astype(F32)
    token_others.append(swapped(tokens[1]))
    while len(tokens) < places:
        tokens.append(send(tokens[-1], upward))
        token_others.append(swapped(tokens[-2]))
    count = len(tokens)
    qkv_turned, gains, up_low_weight, *released = together(
        qkv_turned,
        gains,
        up_low_weight,
        cotangent[0],
        *tokens,
        *token_others,
        *row_sends(gate_low, row_parts, half_flips[1]),
    )
    upstream = [released[0]]
    tokens, token_others = released[1 : 1 + count], list(released[1 + count : 2 * count])
    gate_items = [gate_low, *gate_items, *released[2 * count :]]
    output_full = arrange_output(where, gate_items, query_in, base, width)

    lengths_row = doc_lengths[0]
    doc_ends = jnp.cumsum(lengths_row)
    doc_starts = doc_ends - lengths_row
    positions = jnp.arange(total, dtype=jnp.int32)
    inside = (positions[:, None] >= doc_starts[None, :]) & (positions[:, None] < doc_ends[None, :])
    begins = jnp.sum(jnp.where(inside, doc_starts[None, :], 0), axis=-1)
    angles = rope_rates()[:, None] * (positions - begins).astype(F32)[None, :]
    cos_table, sin_table = jnp.cos(angles), jnp.sin(angles)
    begin_rows = begins.reshape(block_parts, 1, token_count)
    key_rows = 2 * token_count
    last_block = (jnp.arange(block_parts, dtype=jnp.int32) * token_count) // key_rows
    first = begin_rows[:, 0, 0] // key_rows
    full = jnp.clip((begin_rows[:, 0, -1] + key_rows - 1) // key_rows, first, last_block)
    numbers = jnp.arange(block_parts, dtype=jnp.int32)
    order = 2 * ((place - numbers // 2) % places) + (numbers % 2 != me % 2)
    layout = (cos_table, sin_table, begin_rows, order.astype(jnp.int32), first, full)
    sizes = (copies, token_count, key_rows)

    token_others.append(swapped(tokens[-1]))
    held = ()
    for step in range(places):
        held = project(
            step, places, gains[0], qkv_turned, tokens[step], token_others[step], held
        )
    upstream.append(send(upstream[-1], upward))
    upstream[-1], qkv, scaled_first, output_full, *up_items = together(
        upstream[-1],
        held[1],
        held[0],
        output_full,
        *row_sends(up_low_weight, row_parts, half_flips[0]),
    )
    scaled_first = scaled_first.reshape(total, width)
    following = send(upstream[-1], upward)
    saved = attend(qkv, *layout, *sizes)
    following, attended, *last_items = together(
        following, saved[0], *row_sends(up_low_weight, row_parts, half_flips[1])
    )
    upstream.append(following)
    up_items = [up_low_weight, *up_items, *last_items]

    def pair_sums(own_parts, other_parts):
        return [
            low(own.astype(F32) + swapped(other).astype(F32))
            for own, other in zip(own_parts, other_parts)
        ]

    parts = spread_parts(attended, output_full, block_parts)
    while len(upstream) < places:
        upstream.append(send(upstream[-1], upward))
    released = together(*parts, *upstream)
    own_parts, other_parts = released[0 : 2 * places : 2], released[1 : 2 * places : 2]
    upstream = released[2 * places :]
    part, = together(*pair_sums(own_parts[1:2], other_parts[1:2]))
    upstream_others, down_items = [], [down_low]
    for step in range(2, places + 1):
        work = []
        if step == 2:
            work = [
                *pair_sums(own_parts[2:], other_parts[2:]),
                *pair_sums(own_parts[:1], other_parts[:1]),
            ]
        elif step == 3:
            work = [
                *row_sends(down_low, row_parts, half_flips[0]),
                *[swapped(item) for item in upstream[:2]],
            ]
        elif step == 4:
            work = [
                *row_sends(down_low, row_parts, half_flips[1]),
                *[swapped(item) for item in upstream[2:]],
            ]
        arrived, *work = together(send(part, upward), *work)
        if step == 2:
            parts = [work[-1], None, *work[:-1]]
        elif step == 3:
            down_items += work[:-2]
            upstream_others += work[-2:]
        elif step == 4:
            down_items.append(work[0])
            upstream_others += work[1:]
        added = parts[step % places].astype(F32) + arrived.astype(F32)
        part = low(added)
    resid = inputs[0].astype(F32)
    residual = resid + added
    normed_second, inverse_second = norm(residual)

    own = low(normed_second * gains[1])
    own, other = together(own, swapped(own))
    held = ()
    part = carried = None
    result_own, result_other = [], []
    for step in range(places):
        following = send(own, upward) if step + 1 < places else own
        if part is not None:
            carried = send(part, upward)
        outs = feed(
            step,
            places,
            where,
            own,
            other,
            upstream[step],
            upstream_others[step],
            (gate_items, up_items, down_items),
            held,
        )
        held = outs[:5]
        result_own.append(outs[7])
        result_other.append(outs[8])
        released = [following, *outs[5:7]] + ([carried] if part is not None else [])
        released = together(*released)
        own = released[0]
        back_own, back_other = released[1:3]
        fresh = swapped(own) if step + 1 < places else other
        if step == 0:
            last_own, last_other = back_own, back_other
            own, other = together(own, fresh)
        else:
            added = back_own.astype(F32) + swapped(back_other).astype(F32)
            if part is not None:
                added = added + released[3].astype(F32)
            own, other, part = together(own, fresh, low(added))
    second_all, upstream_all, hidden_all, gate_low_all, up_low_all = [
        item.reshape(total, item.shape[2]) for item in held
    ]

    def split_rows(grad):
        size_in, size_out = grad.shape
        return low(grad).reshape(row_parts, size_in // row_parts, size_out)

    def scatter(split):
        return lax.psum_scatter(split, "row", scatter_dimension=0, tiled=True)[0]

    def update(group, gradient):
        return shampoo(gradient, *group)


    carried = send(part, upward)
    last_other = swapped(last_other)
    gate_grad = split_rows(mul_tn(after(second_all, part), gate_low_all))
    carried, last_own, last_other, gate_grad = together(carried, last_own, last_other, gate_grad)
    gate_sum = scatter(gate_grad)
    second_grad = last_own.astype(F32) + last_other.astype(F32) + carried.astype(F32)
    residual_grad = cotangent[0].astype(F32) + norm_back(
        second_grad * gains[1], normed_second, inverse_second
    )
    gain_second_part = jnp.sum(second_grad * normed_second, axis=0)
    residual_low = low(residual_grad)

    first_up = send(residual_low, upward)
    first_down = send(residual_low, downward) if places > 2 else first_up
    up_grad = split_rows(mul_tn(after(second_all, residual_low), up_low_all))
    down_grad = down_gradient(after(hidden_all, residual_low), upstream_all, row_parts)
    out_parts = pair_sums(result_own, result_other)
    first_up, first_down, up_grad, down_grad, *out_parts = together(
        first_up, first_down, up_grad, down_grad, *out_parts
    )
    up_sum = scatter(up_grad)
    down_sum = scatter(down_grad)
    residual_slots = [residual_low, first_up]
    while len(residual_slots) < places - 1:
        residual_slots.append(send(residual_slots[-1], upward))
    if places > 2:
        residual_slots.append(first_down)
    residual_others = [swapped(item) for item in (residual_low, first_up, first_down)]
    gate_update = update(state[4], after(gate_sum, first_up))
    released = together(*residual_slots, *residual_others, *gate_update)
    residual_slots, residual_others = released[:places], list(released[places : places + 3])
    gate_update = released[places + 3 :]
    passed = send(out_parts[1], upward)
    residual_others[2:2] = [swapped(item) for item in residual_slots[2 : places - 1]]
    residual_shards = []
    for pair in zip(residual_slots, residual_others):
        residual_shards += pair
    out_grad, output_grad = output_back(output_full, attended, residual_shards, row_parts)
    out_grad, output_grad, passed = together(out_grad, output_grad, passed)
    hops = 2
    if places > 3:
        passed = send(low(out_parts[hops].astype(F32) + passed.astype(F32)), upward)
        hops += 1
    output_items = row_exchange(output_grad)
    qkv_low = attend_back(saved, out_grad, *layout, *sizes)
    qkv_low, passed, *output_items = together(qkv_low, passed, *output_items)

    while hops < places:
        passed = send(low(out_parts[hops].astype(F32) + passed.astype(F32)), upward)
        hops += 1
    parts = spread_parts(qkv_low, qkv_turned, block_parts)
    query_grad, kv_grad, gain_first_part = projection_grad(
        after(qkv_low, parts[0]), scaled_first, qkv_turned, base, row_parts, block_parts
    )
    query_grad, kv_grad, gain_first_part, passed, *parts = together(
        query_grad, kv_grad, gain_first_part, passed, *parts
    )
    own_parts, other_parts = parts[0::2], parts[1::2]
    part, = together(*pair_sums(own_parts[1:2], other_parts[1:2]))
    result = residual + out_parts[0].astype(F32) + passed.astype(F32)
    gain_parts = jnp.stack([gain_first_part[0] / gains[0, 0], gain_second_part])
    gain_parts = gain_parts.reshape(2, row_parts, block_parts, gain_width).transpose(2, 1, 0, 3)
    gain_parts = low(gain_parts).reshape(block_parts, row_parts, 2 * gain_width)
    gain_parts = jnp.pad(
        gain_parts, ((0, 0), (0, spare - row_parts), (0, head_pair - 2 * gain_width))
    )
    kv_grad = jnp.concatenate([kv_grad, gain_parts], axis=1)

    updates = [None] * 7
    updates[4] = gate_update
    for step in range(2, places + 1):
        work = []
        if step == 2:
            work = [
                lax.all_to_all(kv_grad, "blk", 0, 0),
                *pair_sums(own_parts[2:], other_parts[2:]),
                *pair_sums(own_parts[:1], other_parts[:1]),
                low(result)[None],
                *update(state[5], after(up_sum, part)),
            ]
        elif step == 3:
            kv_back = kv_back.astype(F32)
            gain_back = jnp.sum(kv_back[:, key_in : key_in + row_parts, : 2 * gain_width], axis=0)
            kv_back = kv_back[:, :key_in].reshape(KV_HEADS, shares, key_in, head_pair)
            kv_back = jnp.sum(kv_back, axis=1)
            kv_back = kv_back.reshape(row_parts, key_out // HEAD_DIM, key_in, 2, HEAD_DIM)
            kv_back = kv_back.transpose(0, 3, 2, 1, 4).reshape(row_parts, 2 * key_in, key_out)
            gain_back = jnp.pad(
                gain_back[:, None, :], ((0, 0), (0, spare - 1), (0, key_out - 2 * gain_width))
            )
            kv_back = low(jnp.concatenate([kv_back, gain_back], axis=1))
            work = [
                *row_exchange(kv_back),
                *row_exchange(query_grad),
                *update(state[6], after(down_sum, part)),
            ]
        elif step == 4:
            kv_sum = row_sum(kv_items)
            gains_sum = kv_sum[2 * key_in, : 2 * gain_width].reshape(2, gain_width)
            small = [
                row_sum(query_items),
                kv_sum[:key_in],
                kv_sum[key_in : 2 * key_in],
                row_sum(output_items),
            ]
            for number, gradient in enumerate(small):
                work += update(state[number], after(gradient, part))
        released = together(send(part, upward), *work)
        work = released[1:]
        if step == 2:
            kv_back = work[0]
            first_parts = [work[places - 1], None, *work[1 : places - 1]]
            block_out = work[places]
            updates[5] = work[1 + places :]
        elif step == 3:
            kv_items = work[:row_parts]
            query_items = work[row_parts : 2 * row_parts]
            updates[6] = work[2 * row_parts :]
        elif step == 4:
            for number in range(4):
                updates[number] = work[4 * number : 4 * number + 4]
        added = first_parts[step % places].astype(F32) + released[0].astype(F32)
        part = low(added)
    normed_first, inverse_first = norm(resid)
    input_grad = residual_grad + norm_back(added * gains[0], normed_first, inverse_first)
    outs = [block_out, input_grad[None]]
    for item in updates:
        outs.extend(item)
    outs.extend(adam_step(gains_sum, norm_gains, gain_first, gain_second))
    return tuple(outs)


def solution(mesh):
    tokens_placed = P("row", "blk", None)
    gains_placed = P(None, ("row", "blk"))
    blocks_placed = P(("row", "blk"), None, None)
    return jax.shard_map(
        shards,
        mesh=mesh,
        in_specs=(tokens_placed, tokens_placed, P("row", None))
        + (gains_placed,) * 3
        + (blocks_placed,) * 35,
        out_specs=(tokens_placed,) * 2 + (blocks_placed,) * 28 + (gains_placed,) * 3,
        check_vma=False,
    )
```

time: 4260 us -> 784 us (0.18)
  waiting for transfers between devices: 3220 us -> 290 us
  local copies, waits for them, and re-layouts: 480 us -> 52.2 us
  matrix products: 425 us -> 23.7 us
  Pallas kernels: 0 us -> 268 us
  starting transfers between devices: 1.97 us -> 54.6 us
  blocking collectives: 43 us -> 0 us
    reduce_scatter x9 -> x0, waiting for transfers between devices: 2600 us -> none  [the longest x1 699 us: shards(): lax.psum_scatter(gate_grad, ('row', 'blk'), scatter_dimension=0, tiled=True)]
    all_gather x9 -> x0, waiting for transfers between devices: 620 us -> none  [the longest x1 166 us: shards(): lax.all_gather(gate_weight.astype(jnp.bfloat16), ('row', 'blk'), axis=0,...]
    dot_general x56 -> x2, matrix products: 425 us -> 23.7 us  [mul_tn(): lax.dot_general(left, right, (((0,), (0,)), ((), ())), preferred_element_...]
    ppermute x0 -> x77, waiting for transfers between devices: none -> 269 us  [the longest x24 220 us: send(): return lax.ppermute(array, 'blk', both)]
    pallas_call x0 -> x25, Pallas kernels: none -> 268 us  [the longest x4 99.3 us: feed(): pl.pallas_call(functools.partial(feed_kernel, row_parts), grid_spec=pltpu...]
    reshape x11 -> x3, local copies, waits for them, and re-layouts: 221 us -> 1.7 us  [the longest x1 1.52 us: shards(): kv_back.transpose(0, 3, 2, 1, 4).reshape(row_parts, 2 * key_in, key_out)]
    transpose x4 -> x1, local copies, waits for them, and re-layouts: 188 us -> 1.33 us  [shards(): kv_back.transpose(0, 3, 2, 1, 4).reshape(row_parts, 2 * key_in, key_out)]
    ppermute x0 -> x77, starting transfers between devices: none -> 45 us  [the longest x21 28.2 us: row_send(): return lax.ppermute(array, 'row', [(n, n ^ flip) for n in range(row_parts)])]
  transfers between devices with their start and end apart: 19 -> 82, of which waited for: 17 -> 36; matrix products, arithmetic and copies ran while one was open for 18% -> 13% of each run, Pallas kernels for 0% -> 35%
where the time goes in v1:
time: 784 us; the launch traced here: 774 us
  waiting for transfers between devices  290 us (37%)
  Pallas kernels  268 us (34%)
  other arithmetic  69.3 us (9%)
  starting transfers between devices  54.6 us (7%)
  local copies, waits for them, and re-layouts  52.2 us (7%)
  matrix products  23.7 us (3%)
  between operations  15.8 us (2%)
    ppermute x24, waiting for transfers between devices, send(): return lax.ppermute(array, 'blk', both)  220 us
    pallas_call x4, Pallas kernels, feed(): pl.pallas_call(functools.partial(feed_kernel, row_parts), grid_spec=pltpu...  99.3 us
    convert_element_type x30, other arithmetic, low(): return array.astype(BF16)  45.1 us
    unnamed x245, local copies, waits for them, and re-layouts  39.2 us
    pallas_call x7, Pallas kernels, shampoo(): pl.pallas_call(shampoo_kernel, grid=(steps,), in_specs=[pl.BlockSpec((row...  34.7 us
    pallas_call x1, Pallas kernels, attend_back(): pl.pallas_call(functools.partial(attend_back_kernel, copies, query_rows,...  33.4 us
    ppermute x21, starting transfers between devices, row_send(): return lax.ppermute(array, 'row', [(n, n ^ flip) for n in range(row_parts)])  28.2 us
    ppermute x21, waiting for transfers between devices, row_send(): return lax.ppermute(array, 'row', [(n, n ^ flip) for n in range(row_parts)])  26.9 us
  transfers between devices with their start and end apart: 82, of which 36 were waited for; matrix products, arithmetic and copies ran while one was open for 13% of the time, Pallas kernels for 35%

profile of v1, /device:TPU:0, one launch (start us, length us, event | category | flops | bytes accessed | tf_op | source)
XLA Modules:
  0.0 773.7 jit_solution(13287997449790590262)
XLA Ops:
  53.9 13.7 %collective-permute-done.4.own_ref = bf16[256,2048]{1,0:T(8,128)(2,1)} collective-permute-done((bf16[256,2048]{1,0:T(8,128)(2,1)}, bf16[256,2048]{1,0:T(8,128)(2,1)}, u32[]{:S(2)}, u32[]{:S(2)}) %collective-permute-start.4) | collective-permute-done | bytes 1048608 | tf_op jit(solution)/shard_map/ppermute | solution.py:857
  67.7 9.3 %all-to-all-done.kv_ref = bf16[8,272,128]{2,1,0:T(8,128)(2,1)} async-done(((bf16[8,272,128]{2,1,0:T(8,128)(2,1)}), bf16[8,272,128]{2,1,0:T(8,128)(2,1)}, u32[]{:S(2)}, u32[]{:S(2)}) %all-to-all-start) | async-done | bytes 557088 | tf_op jit(solution)/shard_map/all_to_all | solution.py:939
  83.5 11.9 %collective-permute-done.11.refs_3_ = bf16[640,1024]{1,0:T(8,128)(2,1)} collective-permute-done((bf16[640,1024]{1,0:T(8,128)(2,1)}, bf16[640,1024]{1,0:T(8,128)(2,1)}, u32[]{:S(2)}, u32[]{:S(2)}) %collective-permute-start.11) | collective-permute-done | bytes 1310752 | tf_op jit(solution)/shard_map/ppermute | solution.py:861
  134.9 23.2 %attend.1 = (bf16[256,2048]{1,0:T(8,128)(2,1)S(1)}, bf16[8,64,1024]{2,1,0:T(8,128)(2,1)S(1)}, bf16[2048,64]{1,0:T(8,128)(2,1)S(1)}, bf16[64,2048]{1,0:T(8,128)(2...) custom-call(s32[8]{0:T(128)S(1)} %fusion.18.order_ref, s32[8]{0:T(128)S(1)} %get-tuple-element.599.first_ref, ...), custom_call_target="tpu_custom_call" | custom-call | flops 2147483648 | bytes 8388608 | tf_op jit(solution)/shard_map/attend/pallas_call | solution.py:268
  171.7 16.7 %collective-permute-done.18.grad_own_ref = bf16[256,2048]{1,0:T(8,128)(2,1)S(1)} collective-permute-done((bf16[256,2048]{1,0:T(8,128)(2,1)S(1)}, bf16[256,2048]{1,0:T(8,128)(2,1)S(1)}, u32[]{:S(2)}, u32[]{:S(2)}) %collective-permute-start.18) | collective-permute-done | bytes 1048608 | tf_op jit(solution)/shard_map/ppermute | solution.py:857
  196.8 25.2 %collective-permute-done.20 = bf16[256,2048]{1,0:T(8,128)(2,1)S(1)} collective-permute-done((bf16[256,2048]{1,0:T(8,128)(2,1)S(1)}, bf16[256,2048]{1,0:T(8,128)(2,1)S(1)}, u32[]{:S(2)}, u32[]{:S(2)}) %collective-permute-start.20) | collective-permute-done | bytes 1048608 | tf_op jit(solution)/shard_map/ppermute | solution.py:857
  225.1 23.5 %collective-permute-done.24 = bf16[256,2048]{1,0:T(8,128)(2,1)S(1)} collective-permute-done((bf16[256,2048]{1,0:T(8,128)(2,1)S(1)}, bf16[256,2048]{1,0:T(8,128)(2,1)S(1)}, u32[]{:S(2)}, u32[]{:S(2)}) %collective-permute-start.24) | collective-permute-done | bytes 1048608 | tf_op jit(solution)/shard_map/ppermute | solution.py:857
  249.1 25.2 %collective-permute-done.29 = bf16[256,2048]{1,0:T(8,128)(2,1)S(1)} collective-permute-done((bf16[256,2048]{1,0:T(8,128)(2,1)S(1)}, bf16[256,2048]{1,0:T(8,128)(2,1)S(1)}, u32[]{:S(2)}, u32[]{:S(2)}) %collective-permute-start.29) | collective-permute-done | bytes 1048608 | tf_op jit(solution)/shard_map/ppermute | solution.py:857
  279.2 24.7 %feed.4 = (bf16[4,512,2048]{2,1,0:T(8,128)(2,1)}, bf16[4,512,2048]{2,1,0:T(8,128)(2,1)}, bf16[4,512,1024]{2,1,0:T(8,128)(2,1)}, bf16[4,512,1024]{2,1,0:T(8,128)(...) custom-call(s32[4]{0:T(128)} %iota_xor_fusion.where_ref, ...), custom_call_target="tpu_custom_call" | custom-call | flops 12884901888 | bytes 29360128 | tf_op jit(solution)/shard_map/feed/pallas_call | solution.py:480
  310.1 24.9 %feed.5 = (bf16[4,512,2048]{2,1,0:T(8,128)(2,1)}, bf16[4,512,2048]{2,1,0:T(8,128)(2,1)}, bf16[4,512,1024]{2,1,0:T(8,128)(2,1)}, bf16[4,512,1024]{2,1,0:T(8,128)(...) custom-call(s32[4]{0:T(128)} %iota_xor_fusion.where_ref, ...), custom_call_target="tpu_custom_call", output_to_operand_aliasing={{0}: (17, {}), {1}: (18, {}), {2}: (19, {}), {3}: (20, {}),... | custom-call | flops 12884901888 | bytes 29360128 | tf_op jit(solution)/shard_map/feed/pallas_call | solution.py:480
  342.3 24.9 %feed.6 = (bf16[4,512,2048]{2,1,0:T(8,128)(2,1)}, bf16[4,512,2048]{2,1,0:T(8,128)(2,1)}, bf16[4,512,1024]{2,1,0:T(8,128)(2,1)}, bf16[4,512,1024]{2,1,0:T(8,128)(...) custom-call(s32[4]{0:T(128)} %iota_xor_fusion.where_ref, ...), custom_call_target="tpu_custom_call", output_to_operand_aliasing={{0}: (17, {}), {1}: (18, {}), {2}: (19, {}), {3}: (20, {}),... | custom-call | flops 12884901888 | bytes 29360128 | tf_op jit(solution)/shard_map/feed/pallas_call | solution.py:480
  369.1 21.7 %collective-permute-done.39.own_ref = bf16[256,2048]{1,0:T(8,128)(2,1)} collective-permute-done((bf16[256,2048]{1,0:T(8,128)(2,1)}, bf16[256,2048]{1,0:T(8,128)(2,1)}, u32[]{:S(2)}, u32[]{:S(2)}) %collective-permute-start.39) | collective-permute-done | bytes 1048608 | tf_op jit(solution)/shard_map/ppermute | solution.py:857
  398.6 24.8 %feed.7 = (bf16[4,512,2048]{2,1,0:T(8,128)(2,1)}, bf16[4,512,2048]{2,1,0:T(8,128)(2,1)}, bf16[4,512,1024]{2,1,0:T(8,128)(2,1)}, bf16[4,512,1024]{2,1,0:T(8,128)(...) custom-call(s32[4]{0:T(128)} %iota_xor_fusion.where_ref, ...), custom_call_target="tpu_custom_call", output_to_operand_aliasing={{0}: (17, {}), {1}: (18, {}), {2}: (19, {}), {3}: (20, {}),... | custom-call | flops 12884901888 | bytes 29360128 | tf_op jit(solution)/shard_map/feed/pallas_call | solution.py:480
  431.8 12.8 %convolution_convert_fusion.1 = bf16[2048,1024]{1,0:T(8,128)(2,1)} fusion(bf16[2048,2048]{1,0:T(8,128)(2,1)} %bitcast.142, bf16[2048,1024]{1,0:T(8,128)(2,1)S(1)} %bitcast.146), kind=kOutput, calls=%fused_computation.1 | convolution fusion | flops 8592031744 | bytes 16777216 | tf_op jit(solution)/shard_map/dot_general | solution.py:73
  444.6 14.2 %collective-permute-done.45 = bf16[256,2048]{1,0:T(8,128)(2,1)} collective-permute-done((bf16[256,2048]{1,0:T(8,128)(2,1)S(1)}, bf16[256,2048]{1,0:T(8,128)(2,1)}, u32[]{:S(2)}, u32[]{:S(2)}) %collective-permute-start.45) | collective-permute-done | bytes 1048608 | tf_op jit(solution)/shard_map/ppermute | solution.py:857
  478.4 10.9 %convolution_convert_fusion = bf16[2048,1024]{1,0:T(8,128)(2,1)} fusion(bf16[2048,2048]{1,0:T(8,128)(2,1)S(1)} %bitcast.143, bf16[2048,1024]{1,0:T(8,128)(2,1)S(1)} %bitcast.147), kind=kOutput, calls=%fused_computation | convolution fusion | flops 8592031744 | bytes 16777216 | tf_op jit(solution)/shard_map/dot_general | solution.py:73
  489.3 13.9 %down_gradient.1 = bf16[4,1024,512]{2,1,0:T(8,128)(2,1)S(1)} custom-call(bf16[2048,1024]{1,0:T(8,128)(2,1)} %bitcast.145, bf16[2048,2048]{1,0:T(8,128)(2,1)} %bitcast.144), custom_call_target="tpu_custom_call" | custom-call | flops 8589934592 | bytes 12582912 | tf_op jit(solution)/shard_map/down_gradient/pallas_call | solution.py:749
  505.2 19.2 %collective-permute-done.48.refs_6_ = bf16[256,2048]{1,0:T(8,128)(2,1)S(1)} collective-permute-done((bf16[256,2048]{1,0:T(8,128)(2,1)}, bf16[256,2048]{1,0:T(8,128)(2,1)S(1)}, u32[]{:S(2)}, u32[]{:S(2)}) %collective-permute-start.48) | collective-permute-done | bytes 1048608 | tf_op jit(solution)/shard_map/ppermute | solution.py:857
  539.3 14.8 %collective-permute-done.53.refs_4_ = bf16[256,2048]{1,0:T(8,128)(2,1)} collective-permute-done((bf16[256,2048]{1,0:T(8,128)(2,1)}, bf16[256,2048]{1,0:T(8,128)(2,1)}, u32[]{:S(2)}, u32[]{:S(2)}) %collective-permute-start.53) | collective-permute-done | bytes 1048608 | tf_op jit(solution)/shard_map/ppermute | solution.py:857
  557.9 9.8 %output_back.1 = (bf16[256,2048]{1,0:T(8,128)(2,1)S(1)}, bf16[4,256,512]{2,1,0:T(8,128)(2,1)}) custom-call(bf16[256,2048]{1,0:T(8,128)(2,1)} %arrange_output.1.weight_ref, bf16[256,2048]{1,0:T(8,128)(2,1)} %copy-done.55, bf16[256,2048]{1,0:T(8,128)(2,1)} %get-tuple-element.464.refs_0_, bf16[256,2048]{1,0:T(8,128)(2,1)} %collective-permute-done.54.refs_1_, ...), custom_call_target="tpu_custom_call" | custom-call | flops 4294967296 | bytes 8388608 | tf_op jit(solution)/shard_map/output_back/pallas_call | solution.py:826
  567.8 14.1 %collective-permute-done.58 = bf16[256,2048]{1,0:T(8,128)(2,1)S(1)} collective-permute-done((bf16[256,2048]{1,0:T(8,128)(2,1)}, bf16[256,2048]{1,0:T(8,128)(2,1)S(1)}, u32[]{:S(2)}, u32[]{:S(2)}) %collective-permute-start.58) | collective-permute-done | bytes 1048608 | tf_op jit(solution)/shard_map/ppermute | solution.py:857
  591.5 33.4 %attend_back.1.rows_ref.grads_ref = bf16[384,2048]{1,0:T(8,128)(2,1)} custom-call(s32[8]{0:T(128)S(1)} %fusion.18.order_ref, s32[8]{0:T(128)S(1)} %get-tuple-element.599.first_ref, s32[8]{0:T(128)S(1)} %get-tuple-element.598.full_ref, s32[8,1,256]{2,1,0:T(1,128)S(1)} %bitcast.110, bf16[8,64,1024]{2,1,0:T(8,128)(2,1)S(1)} %copy-done.58, ...), custom_call_target="tpu_custom_call" | custom-call | flops 5368709120 | bytes 8388608 | tf_op jit(solution)/shard_map/attend_back/pallas_call | solution.py:317
  627.2 11.3 %spread.3 = (bf16[256,2048]{1,0:T(8,128)(2,1)S(1)}, bf16[256,2048]{1,0:T(8,128)(2,1)}, bf16[256,2048]{1,0:T(8,128)(2,1)S(1)}, bf16[256,2048]{1,0:T(8,128)(2,1)},...) custom-call(bf16[384,2048]{1,0:T(8,128)(2,1)} %attend_back.1.rows_re, ...), custom_call_target="tpu_custom_call" | custom-call | flops 3221225472 | bytes 8388608 | tf_op jit(solution)/shard_map/spread/pallas_call | solution.py:786
  686.5 11.6 %all-to-all-done.1 = bf16[8,272,128]{2,1,0:T(8,128)(2,1)} async-done(((bf16[8,272,128]{2,1,0:T(8,128)(2,1)}), bf16[8,272,128]{2,1,0:T(8,128)(2,1)}, u32[]{:S(2)}, u32[]{:S(2)}) %all-to-all-start.1) | async-done | bytes 557088 | tf_op jit(solution)/shard_map/all_to_all | solution.py:1181
  (504 shorter events, 322.1 us)
Async XLA Ops:
  35.8 41.2 %collective-permute-start.6 = (bf16[640,1024]{1,0:T(8,128)(2,1)}, bf16[640,1024]{1,0:T(8,128)(2,1)}, u32[]{:S(2)}, u32[]{:S(2)}) collective-permute-start(bf16[640,1024]{1,0:T(8,128)(2,1)} %maximum_maximum_fusion.refs_0_), channel_id=1, source_target_pairs={{0,16},{8,24},{16,0},{24,8},{1,17},{9,25},{17,1},{25,9},{2,18},{10... | collective-permute-start | bytes 3932168 | tf_op jit(solution)/shard_map/ppermute | solution.py:861
  37.3 39.7 %collective-permute-start.5 = (bf16[640,1024]{1,0:T(8,128)(2,1)}, bf16[640,1024]{1,0:T(8,128)(2,1)}, u32[]{:S(2)}, u32[]{:S(2)}) collective-permute-start(bf16[640,1024]{1,0:T(8,128)(2,1)} %maximum_maximum_fusion.refs_0_), channel_id=1, source_target_pairs={{0,8},{8,0},{16,24},{24,16},{1,9},{9,1},{17,25},{25,17},{2,10},{10... | collective-permute-start | bytes 3932168 | tf_op jit(solution)/shard_map/ppermute | solution.py:861
  44.2 32.8 %all-to-all-start = ((bf16[8,272,128]{2,1,0:T(8,128)(2,1)}), bf16[8,272,128]{2,1,0:T(8,128)(2,1)}, u32[]{:S(2)}, u32[]{:S(2)}) async-start(bf16[8,272,128]{2,1,0:T(8,128)(2,1)} %split_entry.1), calls=%async_computation | async-start | bytes 1114112 | tf_op jit(solution)/shard_map/all_to_all | solution.py:939
  49.3 477.2 %reduce-scatter.10.cloned.1.call-start = ((), (), s32[]{:S(2)}) async-start(), calls=%async_computation.5 | async-start | bytes 5242880
  49.4 33.1 %collective-permute-start.8 = (bf16[256,2048]{1,0:T(8,128)(2,1)S(1)}, bf16[256,2048]{1,0:T(8,128)(2,1)}, u32[]{:S(2)}, u32[]{:S(2)}) collective-permute-start(bf16[256,2048]{1,0:T(8,128)(2,1)S(1)} %bitcast.100), channel_id=1, source_target_pairs={{0,1},{1,0},{2,3},{3,2},{4,5},{5,4},{6,7},{7,6},{8,9},{9,8},{10,11... | collective-permute-start | bytes 3145736 | tf_op jit(solution)/shard_map/ppermute | solution.py:914
  52.3 43.0 %collective-permute-start.11 = (bf16[640,1024]{1,0:T(8,128)(2,1)}, bf16[640,1024]{1,0:T(8,128)(2,1)}, u32[]{:S(2)}, u32[]{:S(2)}) collective-permute-start(bf16[640,1024]{1,0:T(8,128)(2,1)} %maximum_maximum_fusion.refs_0_), channel_id=1, source_target_pairs={{0,24},{8,16},{16,8},{24,0},{1,25},{9,17},{17,9},{25,1},{2,26},{10... | collective-permute-start | bytes 3932168 | tf_op jit(solution)/shard_map/ppermute | solution.py:861
  106.7 55.7 %collective-permute-start.17 = (bf16[512,1024]{1,0:T(8,128)(2,1)}, bf16[512,1024]{1,0:T(8,128)(2,1)}, u32[]{:S(2)}, u32[]{:S(2)}) collective-permute-start(bf16[512,1024]{1,0:T(8,128)(2,1)} %convert_bitcast_fusion.refs_4_), channel_id=1, source_target_pairs={{0,24},{8,16},{16,8},{24,0},{1,25},{9,17},{17,9},{25,1},{2,26},{10... | collective-permute-start | bytes 3145736 | tf_op jit(solution)/shard_map/ppermute | solution.py:861
  133.3 29.1 %collective-permute-start.16 = (bf16[256,2048]{1,0:T(8,128)(2,1)}, bf16[256,2048]{1,0:T(8,128)(2,1)S(1)}, u32[]{:S(2)}, u32[]{:S(2)}) collective-permute-start(bf16[256,2048]{1,0:T(8,128)(2,1)} %collective-permute-done.12.grad_own_ref), channel_id=1, source_target_pairs={{0,2},{1,3},{2,4},{3,5},{4,6},{5,7},{6,0},{7,1},{8,10},{9,11},{10,... | collective-permute-start | bytes 3145736 | tf_op jit(solution)/shard_map/ppermute | solution.py:857
  188.9 33.5 %collective-permute-start.26 = (bf16[512,1024]{1,0:T(8,128)(2,1)S(1)}, bf16[512,1024]{1,0:T(8,128)(2,1)S(1)}, u32[]{:S(2)}, u32[]{:S(2)}) collective-permute-start(bf16[512,1024]{1,0:T(8,128)(2,1)S(1)} %bitcast.124), channel_id=1, source_target_pairs={{0,16},{8,24},{16,0},{24,8},{1,17},{9,25},{17,1},{25,9},{2,18},{10... | collective-permute-start | bytes 3145736 | tf_op jit(solution)/shard_map/ppermute | solution.py:861
  190.6 33.8 %collective-permute-start.25 = (bf16[512,1024]{1,0:T(8,128)(2,1)S(1)}, bf16[512,1024]{1,0:T(8,128)(2,1)S(1)}, u32[]{:S(2)}, u32[]{:S(2)}) collective-permute-start(bf16[512,1024]{1,0:T(8,128)(2,1)S(1)} %bitcast.125), channel_id=1, source_target_pairs={{0,8},{8,0},{16,24},{24,16},{1,9},{9,1},{17,25},{25,17},{2,10},{10... | collective-permute-start | bytes 3145736 | tf_op jit(solution)/shard_map/ppermute | solution.py:861
  193.1 31.4 %collective-permute-start.27 = (bf16[256,2048]{1,0:T(8,128)(2,1)S(1)}, bf16[256,2048]{1,0:T(8,128)(2,1)S(1)}, u32[]{:S(2)}, u32[]{:S(2)}) collective-permute-start(bf16[256,2048]{1,0:T(8,128)(2,1)S(1)} %bitcast.119), channel_id=1, source_target_pairs={{0,1},{1,0},{2,3},{3,2},{4,5},{5,4},{6,7},{7,6},{8,9},{9,8},{10,11... | collective-permute-start | bytes 3145736 | tf_op jit(solution)/shard_map/ppermute | solution.py:914
  196.2 28.8 %collective-permute-start.28 = (bf16[256,2048]{1,0:T(8,128)(2,1)}, bf16[256,2048]{1,0:T(8,128)(2,1)S(1)}, u32[]{:S(2)}, u32[]{:S(2)}) collective-permute-start(bf16[256,2048]{1,0:T(8,128)(2,1)} %collective-permute-done.12.grad_own_ref), channel_id=1, source_target_pairs={{0,1},{1,0},{2,3},{3,2},{4,5},{5,4},{6,7},{7,6},{8,9},{9,8},{10,11... | collective-permute-start | bytes 3145736 | tf_op jit(solution)/shard_map/ppermute | solution.py:914
  342.1 48.7 %collective-permute-start.39 = (bf16[256,2048]{1,0:T(8,128)(2,1)}, bf16[256,2048]{1,0:T(8,128)(2,1)}, u32[]{:S(2)}, u32[]{:S(2)}) collective-permute-start(bf16[256,2048]{1,0:T(8,128)(2,1)} %collective-permute-done.36.own_ref), channel_id=1, source_target_pairs={{0,2},{1,3},{2,4},{3,5},{4,6},{5,7},{6,0},{7,1},{8,10},{9,11},{10,... | collective-permute-start | bytes 3145736 | tf_op jit(solution)/shard_map/ppermute | solution.py:857
  458.9 209.1 %reduce-scatter.12.cloned.1.call-start = ((), (), s32[]{:S(2)}) async-start(), calls=%async_computation.6 | async-start | bytes 5242880
  476.3 48.1 %collective-permute-start.48 = (bf16[256,2048]{1,0:T(8,128)(2,1)}, bf16[256,2048]{1,0:T(8,128)(2,1)S(1)}, u32[]{:S(2)}, u32[]{:S(2)}) collective-permute-start(bf16[256,2048]{1,0:T(8,128)(2,1)} %get-tuple-element.464.refs_0_), channel_id=1, source_target_pairs={{0,6},{1,7},{2,0},{3,1},{4,2},{5,3},{6,4},{7,5},{8,14},{9,15},{10,... | collective-permute-start | bytes 3145736 | tf_op jit(solution)/shard_map/ppermute | solution.py:857
  476.3 48.1 %collective-permute-start.47 = (bf16[256,2048]{1,0:T(8,128)(2,1)}, bf16[256,2048]{1,0:T(8,128)(2,1)S(1)}, u32[]{:S(2)}, u32[]{:S(2)}) collective-permute-start(bf16[256,2048]{1,0:T(8,128)(2,1)} %get-tuple-element.464.refs_0_), channel_id=1, source_target_pairs={{0,2},{1,3},{2,4},{3,5},{4,6},{5,7},{6,0},{7,1},{8,10},{9,11},{10,... | collective-permute-start | bytes 3145736 | tf_op jit(solution)/shard_map/ppermute | solution.py:857
  525.8 188.1 %reduce-scatter.14.cloned.1.call-start = ((), (), s32[]{:S(2)}) async-start(), calls=%async_computation.7 | async-start | bytes 5242880
  585.6 39.4 %collective-permute-start.59 = (bf16[256,2048]{1,0:T(8,128)(2,1)}, bf16[256,2048]{1,0:T(8,128)(2,1)}, u32[]{:S(2)}, u32[]{:S(2)}) collective-permute-start(bf16[256,2048]{1,0:T(8,128)(2,1)} %add_convert_fusion.8), channel_id=1, source_target_pairs={{0,2},{1,3},{2,4},{3,5},{4,6},{5,7},{6,0},{7,1},{8,10},{9,11},{10,... | collective-permute-start | bytes 3145736 | tf_op jit(solution)/shard_map/ppermute | solution.py:857
  588.0 37.0 %collective-permute-start.62 = (bf16[256,512]{1,0:T(8,128)(2,1)S(1)}, bf16[256,512]{1,0:T(8,128)(2,1)S(1)}, u32[]{:S(2)}, u32[]{:S(2)}) collective-permute-start(bf16[256,512]{1,0:T(8,128)(2,1)S(1)} %get-tuple-element.605), channel_id=1, source_target_pairs={{0,24},{8,16},{16,8},{24,0},{1,25},{9,17},{17,9},{25,1},{2,26},{10... | collective-permute-start | bytes 786440 | tf_op jit(solution)/shard_map/ppermute | solution.py:861
  589.6 35.4 %collective-permute-start.61 = (bf16[256,512]{1,0:T(8,128)(2,1)S(1)}, bf16[256,512]{1,0:T(8,128)(2,1)S(1)}, u32[]{:S(2)}, u32[]{:S(2)}) collective-permute-start(bf16[256,512]{1,0:T(8,128)(2,1)S(1)} %get-tuple-element.606), channel_id=1, source_target_pairs={{0,16},{8,24},{16,0},{24,8},{1,17},{9,25},{17,1},{25,9},{2,18},{10... | collective-permute-start | bytes 786440 | tf_op jit(solution)/shard_map/ppermute | solution.py:861
  589.8 35.2 %collective-permute-start.60 = (bf16[256,512]{1,0:T(8,128)(2,1)S(1)}, bf16[256,512]{1,0:T(8,128)(2,1)S(1)}, u32[]{:S(2)}, u32[]{:S(2)}) collective-permute-start(bf16[256,512]{1,0:T(8,128)(2,1)S(1)} %get-tuple-element.607), channel_id=1, source_target_pairs={{0,8},{8,0},{16,24},{24,16},{1,9},{9,1},{17,25},{25,17},{2,10},{10... | collective-permute-start | bytes 786440 | tf_op jit(solution)/shard_map/ppermute | solution.py:861
  655.4 42.7 %all-to-all-start.1 = ((bf16[8,272,128]{2,1,0:T(8,128)(2,1)}), bf16[8,272,128]{2,1,0:T(8,128)(2,1)}, u32[]{:S(2)}, u32[]{:S(2)}) async-start(bf16[8,272,128]{2,1,0:T(8,128)(2,1)} %fusion.13), calls=%async_computation.1 | async-start | bytes 1114112 | tf_op jit(solution)/shard_map/all_to_all | solution.py:1181
  666.4 31.7 %collective-permute-start.65 = (bf16[256,2048]{1,0:T(8,128)(2,1)}, bf16[256,2048]{1,0:T(8,128)(2,1)}, u32[]{:S(2)}, u32[]{:S(2)}) collective-permute-start(bf16[256,2048]{1,0:T(8,128)(2,1)} %add_convert_fusion.6), channel_id=1, source_target_pairs={{0,2},{1,3},{2,4},{3,5},{4,6},{5,7},{6,0},{7,1},{8,10},{9,11},{10,... | collective-permute-start | bytes 3145736 | tf_op jit(solution)/shard_map/ppermute | solution.py:857
  700.8 31.4 %collective-permute-start.69 = (bf16[256,2048]{1,0:T(8,128)(2,1)}, bf16[256,2048]{1,0:T(8,128)(2,1)}, u32[]{:S(2)}, u32[]{:S(2)}) collective-permute-start(bf16[256,2048]{1,0:T(8,128)(2,1)} %add_convert_fusion.1), channel_id=1, source_target_pairs={{0,2},{1,3},{2,4},{3,5},{4,6},{5,7},{6,0},{7,1},{8,10},{9,11},{10,... | collective-permute-start | bytes 3145736 | tf_op jit(solution)/shard_map/ppermute | solution.py:857
  (180 other events, 2196.2 us)
Sparse Core Ops, SparseCore 0:
  459.0 50.4 reduce-scatter.9
  525.9 50.6 reduce-scatter.11
  580.1 63.9 reduce-scatter.13
